TPU v7x, 768 devices: a whole 4x8x12 slice. The times are simulated.
768 devices in a mesh: tm: 96 (over x, z, y_lo), space: 8 (over y_hi, core).
Axes of the slice: x: 4, y: 8 (y_hi: 4, y_lo: 2; y = y_hi * 2 + y_lo), z: 12, core: 2. Of those that a mesh axis runs over, the one named last changes fastest.
Arguments:
- state_field: float32 [96, 64, 12, 128], P('tm', 'space'), may hold values from -6 to 6
- adjoint: float32 [96, 64, 12, 128], P('tm', 'space'), may hold values from -6 to 6
- target: float32 [96, 64, 12, 128], P('tm', 'space'), may hold values from -4 to 4
- conductivity: float32 [64, 12, 128], P('space'), may hold values from 0.2 to 2
Outputs:
- residual_state: float32 [96, 64, 12, 128], P('tm', 'space')
- residual_adjoint: float32 [96, 64, 12, 128], P('tm', 'space')
- spectral_correction: float32 [4, 96, 64, 1536], P(None, None, 'space', 'tm')
All inputs are finite; a program needn't handle non-finite values.
Results may differ from a plain program's by a relative error of at most 0.00013.
Values sent between devices are 32-bit elements; how exact they have to be, the bound alone decides.
A program may use at most 32 MiB of HBM per device.

v0:
```python
import math

import jax
import jax.numpy as jnp
from jax import lax
from jax.sharding import PartitionSpec as P

diffusion = 0.05
control_cost = 0.2
tracking = 0.5


def padded(shard, sides, width):
    for axis, dim in sides:
        count, length = (lax.axis_size(axis), shard.shape[dim])
        up = [(i, (i + 1) % count) for i in range(count - 1)]
        down = [(j, i) for i, j in up]
        last = lax.slice_in_dim(shard, length - width, length, axis=dim)
        leading = lax.slice_in_dim(shard, 0, width, axis=dim)
        before = lax.ppermute(last, axis, up)
        after = lax.ppermute(leading, axis, down)
        shard = jnp.concatenate([before, shard, after], axis=dim)
    return shard


def shifted(value, axis, steps):
    count = lax.axis_size(axis)
    pairs = [(source, (source + steps) % count) for source in range(count)]
    return lax.ppermute(value, axis, pairs)


def plane_sum(values_in):
    zero_row = jnp.zeros_like(values_in[..., :1, :])
    along_x = jnp.concatenate([values_in[..., 1:, :], zero_row], axis=-2) + jnp.concatenate(
        [zero_row, values_in[..., :-1, :]], axis=-2
    )
    zero_col = jnp.zeros_like(values_in[..., :1])
    along_y = jnp.concatenate([values_in[..., 1:], zero_col], axis=-1) + jnp.concatenate(
        [zero_col, values_in[..., :-1]], axis=-1
    )
    return along_x + along_y


def shards(state_field, adjoint, target, conductivity):
    weighted = conductivity[None] * adjoint
    stacked = jnp.stack([state_field, weighted])
    planes = padded(stacked, (("space", 2),), 1)
    state_prev = shifted(state_field, "tm", 1)
    adjoint_next = shifted(adjoint, "tm", -1)
    centre = planes[:, :, 1:-1]
    beside_all = planes[:, :, :-2] + planes[:, :, 2:] + plane_sum(centre)
    diffused_state = conductivity[None] * (6.0 * state_field - beside_all[0])
    diffused_adjoint = 6.0 * weighted - beside_all[1]
    residual_state = state_field - state_prev + diffusion * diffused_state - control_cost * adjoint
    residual_adjoint = (
        adjoint - adjoint_next + diffusion * diffused_adjoint + tracking * (state_field - target)
    )
    slab_depth = state_field.shape[1]
    plane_cells = state_field.shape[2] * state_field.shape[3]
    step_count = lax.axis_size("tm")
    share_size = plane_cells // step_count
    flat_state = residual_state.reshape(1, slab_depth, plane_cells)
    flat_adjoint = residual_adjoint.reshape(1, slab_depth, plane_cells)
    got_state, got_adjoint = (
        lax.all_to_all(flat_state, "tm", split_axis=2, concat_axis=0, tiled=True),
        lax.all_to_all(flat_adjoint, "tm", split_axis=2, concat_axis=0, tiled=True),
    )
    owned_cond = lax.dynamic_slice_in_dim(
        conductivity.reshape(slab_depth, plane_cells),
        lax.axis_index("tm") * share_size,
        share_size,
        1,
    )
    step_index = jnp.arange(step_count, dtype=jnp.int32)
    angles = (step_index[:, None] * step_index[None, :] % step_count).astype(jnp.float32) * (
        2.0 * math.pi / step_count
    )
    dft_table = jnp.concatenate([jnp.cos(angles), -jnp.sin(angles)], axis=0) * (
        1.0 / math.sqrt(step_count)
    )
    stacked_res = jnp.stack([got_state, got_adjoint], axis=1).reshape(
        step_count, 2 * slab_depth * share_size
    )
    spectra = jnp.dot(
        dft_table, stacked_res, precision=lax.Precision.HIGHEST, preferred_element_type=jnp.float32
    )
    spectra = spectra.reshape(2, step_count, 2, slab_depth, share_size)
    state_real = spectra[0, :, 0]
    adjoint_real = spectra[0, :, 1]
    state_imag = spectra[1, :, 0]
    adjoint_imag = spectra[1, :, 1]
    unit_angle = angles[:, 1]
    cosine_step = jnp.cos(unit_angle)[:, None, None]
    sine_step = jnp.sin(unit_angle)[:, None, None]
    diagonal_term = 1.0 + diffusion * 6.0 * owned_cond[None] - cosine_step
    determinant = diagonal_term * diagonal_term + sine_step * sine_step + control_cost * tracking
    fix_state_real = (
        diagonal_term * state_real + sine_step * state_imag + control_cost * adjoint_real
    ) / determinant
    fix_state_imag = (
        diagonal_term * state_imag - sine_step * state_real + control_cost * adjoint_imag
    ) / determinant
    fix_adjoint_real = (
        diagonal_term * adjoint_real - sine_step * adjoint_imag - tracking * state_real
    ) / determinant
    fix_adjoint_imag = (
        diagonal_term * adjoint_imag + sine_step * adjoint_real - tracking * state_imag
    ) / determinant
    spectral_correction = jnp.stack(
        [fix_state_real, fix_state_imag, fix_adjoint_real, fix_adjoint_imag]
    )
    return (residual_state, residual_adjoint, spectral_correction)


def solution(mesh):
    placed = (
        P("tm", "space", None, None),
        P("tm", "space", None, None),
        P("tm", "space", None, None),
        P("space", None, None),
    )
    return jax.shard_map(
        shards,
        mesh=mesh,
        in_specs=placed,
        out_specs=(
            P("tm", "space", None, None),
            P("tm", "space", None, None),
            P(None, None, "space", "tm"),
        ),
        check_vma=False,
    )
```

profile of v0, /device:TPU:17, one launch (start us, length us, event | category | flops | bytes accessed | tf_op | source)
XLA Modules:
  0.0 88.3 jit_solution(6473737194187706329)
XLA Ops:
  0.6 0.0 copy-start
  0.6 3.3 %collective-permute-start = (f32[1,8,12,128]{3,1,2,0:T(8,128)}, f32[1,8,12,128]{3,1,2,0:T(8,128)S(1)}, u32[]{:S(2)}, u32[]{:S(2)}) collective-permute-start(f32[1,8,12,128]{3,1,2,0:T(8,128)} %param.4), channel_id=1, source_target_pairs={{0,8},{8,16},{16,24},{24,32},{32,40},{40,48},{48,56},{56,64},{64,7... | collective-permute-start | bytes 147464 | tf_op jit(solution)/shard_map/ppermute | solution.py:29
  4.0 16.2 %collective-permute-start.3 = (f32[1,8,12,128]{3,1,2,0:T(8,128)}, f32[1,8,12,128]{3,1,2,0:T(8,128)S(1)}, u32[]{:S(2)}, u32[]{:S(2)}) collective-permute-start(f32[1,8,12,128]{3,1,2,0:T(8,128)} %param.5), channel_id=1, source_target_pairs={{0,760},{8,0},{16,8},{24,16},{32,24},{40,32},{48,40},{56,48},{64,5... | collective-permute-start | bytes 147464 | tf_op jit(solution)/shard_map/ppermute | solution.py:29
  20.2 0.8 fusion.39
  21.1 0.0 copy-done
  21.1 5.4 %collective-permute-start.1 = (f32[2,1,1,12,128]{4,2,3,1,0:T(1,128)S(1)}, f32[2,1,1,12,128]{4,2,3,1,0:T(1,128)S(1)}, u32[]{:S(2)}, u32[]{:S(2)}) collective-permute-start(f32[2,1,1,12,128]{4,2,3,1,0:T(1,128)S(1)} %get-tuple-element.11), channel_id=1, source_target_pairs={{0,1},{1,2},{2,3},{3,4},{4,5},{5,6},{6,7},{8,9},{9,10},{10,11},{11... | collective-permute-start | bytes 36872 | tf_op jit(solution)/shard_map/ppermute | solution.py:20
  26.5 1.9 %collective-permute-start.2 = (f32[2,1,1,12,128]{4,2,3,1,0:T(1,128)S(1)}, f32[2,1,1,12,128]{4,2,3,1,0:T(1,128)S(1)}, u32[]{:S(2)}, u32[]{:S(2)}) collective-permute-start(f32[2,1,1,12,128]{4,2,3,1,0:T(1,128)S(1)} %get-tuple-element.12), channel_id=1, source_target_pairs={{1,0},{2,1},{3,2},{4,3},{5,4},{6,5},{7,6},{9,8},{10,9},{11,10},{12... | collective-permute-start | bytes 36872 | tf_op jit(solution)/shard_map/ppermute | solution.py:21
  28.5 0.1 fusion.3
  28.6 0.0 collective-permute-done.1
  28.6 5.0 %collective-permute-done.2 = f32[2,1,1,12,128]{4,2,3,1,0:T(1,128)S(1)} collective-permute-done((f32[2,1,1,12,128]{4,2,3,1,0:T(1,128)S(1)}, f32[2,1,1,12,128]{4,2,3,1,0:T(1,128)S(1)}, u32[]{:S(2)}, u32[]{:S(2)}) %collective-permute-start.2) | collective-permute-done | bytes 12320 | tf_op jit(solution)/shard_map/ppermute | solution.py:21
  33.6 0.0 copy-start.1
  33.6 0.0 copy-start.4
  33.6 0.1 fusion.6
  33.7 0.0 collective-permute-done
  33.7 0.0 collective-permute-done.3
  33.7 0.7 copy-done.1
  34.4 0.0 copy-done.4
  34.4 0.0 copy-done.5
  34.5 0.0 copy-start.3
  34.5 0.0 copy-start.2
  34.5 0.3 copy.12
  34.8 0.3 copy-done.3
  35.1 0.6 broadcast.183
  35.7 7.1 %reduce.2 = f32[1536,8]{1,0:T(8,128)S(1)} reduce(f32[1536,1,8]{2,1,0:T(1,128)S(1)} %bitcast.96, f32[]{:T(128)} %broadcast.183), dimensions={1}, to_apply=%bitcast.93.reduce_sub_computation | reduce | bytes 98308
  42.8 1.0 %reshape.227 = f32[96,1,128]{2,1,0:T(1,128)} reshape(f32[1536,8]{1,0:T(8,128)S(1)} %reduce.2) | data formatting | bytes 98304
  43.8 6.9 %all-to-all-start = ((f32[96,1,128]{2,1,0:T(1,128)}), f32[96,1,128]{2,1,0:T(1,128)S(1)}, u32[]{:S(2)}, u32[]{:S(2)}) async-start(f32[96,1,128]{2,1,0:T(1,128)} %reshape.227), calls=%async_computation | async-start | bytes 98304 | tf_op jit(solution)/shard_map/all_to_all | solution.py:65
  50.7 0.2 sine_negate_fusion
  51.0 0.0 copy-done.2
  51.0 0.3 copy.14
  51.3 7.2 %reduce = f32[1536,8]{1,0:T(8,128)S(1)} reduce(f32[1536,1,8]{2,1,0:T(1,128)S(1)} %bitcast.99, f32[]{:T(128)} %broadcast.183), dimensions={1}, to_apply=%bitcast.91.reduce_sub_computation | reduce | bytes 98308
  58.4 1.0 %reshape.225 = f32[96,1,128]{2,1,0:T(1,128)} reshape(f32[1536,8]{1,0:T(8,128)S(1)} %reduce) | data formatting | bytes 98304
  59.4 2.9 %all-to-all-done = f32[96,1,128]{2,1,0:T(1,128)S(1)} async-done(((f32[96,1,128]{2,1,0:T(1,128)}), f32[96,1,128]{2,1,0:T(1,128)S(1)}, u32[]{:S(2)}, u32[]{:S(2)}) %all-to-all-start) | async-done | bytes 49184 | tf_op jit(solution)/shard_map/all_to_all | solution.py:65
  62.3 10.9 %all-to-all-start.1 = ((f32[96,1,128]{2,1,0:T(1,128)}), f32[96,1,128]{2,1,0:T(1,128)S(1)}, u32[]{:S(2)}, u32[]{:S(2)}) async-start(f32[96,1,128]{2,1,0:T(1,128)} %reshape.225), calls=%async_computation.1 | async-start | bytes 98304 | tf_op jit(solution)/shard_map/all_to_all | solution.py:66
  73.2 0.1 maximum_multiply_fusion
  73.3 0.1 copy.11
  73.4 0.1 multiply_add_fusion
  73.5 0.7 reduce.3
  74.3 1.2 %reshape.228 = f32[1536,1,8]{2,1,0:T(1,128)S(1)} reshape(f32[96,128]{1,0:T(8,128)S(1)} %reduce.3) | data formatting | bytes 98304
  75.5 0.3 copy.19
  75.8 0.1 copy.16
  75.9 8.6 %all-to-all-done.1 = f32[96,1,128]{2,1,0:T(1,128)S(1)} async-done(((f32[96,1,128]{2,1,0:T(1,128)}), f32[96,1,128]{2,1,0:T(1,128)S(1)}, u32[]{:S(2)}, u32[]{:S(2)}) %all-to-all-start.1) | async-done | bytes 49184 | tf_op jit(solution)/shard_map/all_to_all | solution.py:66
  84.6 0.7 reduce.1
  85.3 1.2 %reshape.226 = f32[1536,1,8]{2,1,0:T(1,128)S(1)} reshape(f32[96,128]{1,0:T(8,128)S(1)} %reduce.1) | data formatting | bytes 98304
  86.5 0.3 copy.20
  86.8 0.1 copy.17
  87.0 0.4 fusion
  87.4 0.1 fusion.12
  87.5 0.7 pad_maximum_fusion
  (7 shorter events, 0.2 us)
Async XLA Ops:
  0.6 20.4 %copy-start = (f32[1,8,12,128]{3,1,2,0:T(8,128)S(1)}, f32[1,8,12,128]{3,1,2,0:T(8,128)}, u32[]{:S(2)}) copy-start(f32[1,8,12,128]{3,1,2,0:T(8,128)} %param.4) | copy-start | bytes 147460
  0.6 33.1 %collective-permute-start = (f32[1,8,12,128]{3,1,2,0:T(8,128)}, f32[1,8,12,128]{3,1,2,0:T(8,128)S(1)}, u32[]{:S(2)}, u32[]{:S(2)}) collective-permute-start(f32[1,8,12,128]{3,1,2,0:T(8,128)} %param.4), channel_id=1, source_target_pairs={{0,8},{8,16},{16,24},{24,32},{32,40},{40,48},{48,56},{56,64},{64,7... | collective-permute-start | bytes 147464 | tf_op jit(solution)/shard_map/ppermute | solution.py:29
  4.0 29.7 %collective-permute-start.3 = (f32[1,8,12,128]{3,1,2,0:T(8,128)}, f32[1,8,12,128]{3,1,2,0:T(8,128)S(1)}, u32[]{:S(2)}, u32[]{:S(2)}) collective-permute-start(f32[1,8,12,128]{3,1,2,0:T(8,128)} %param.5), channel_id=1, source_target_pairs={{0,760},{8,0},{16,8},{24,16},{32,24},{40,32},{48,40},{56,48},{64,5... | collective-permute-start | bytes 147464 | tf_op jit(solution)/shard_map/ppermute | solution.py:29
  21.1 7.5 %collective-permute-start.1 = (f32[2,1,1,12,128]{4,2,3,1,0:T(1,128)S(1)}, f32[2,1,1,12,128]{4,2,3,1,0:T(1,128)S(1)}, u32[]{:S(2)}, u32[]{:S(2)}) collective-permute-start(f32[2,1,1,12,128]{4,2,3,1,0:T(1,128)S(1)} %get-tuple-element.11), channel_id=1, source_target_pairs={{0,1},{1,2},{2,3},{3,4},{4,5},{5,6},{6,7},{8,9},{9,10},{10,11},{11... | collective-permute-start | bytes 36872 | tf_op jit(solution)/shard_map/ppermute | solution.py:20
  26.5 7.1 %collective-permute-start.2 = (f32[2,1,1,12,128]{4,2,3,1,0:T(1,128)S(1)}, f32[2,1,1,12,128]{4,2,3,1,0:T(1,128)S(1)}, u32[]{:S(2)}, u32[]{:S(2)}) collective-permute-start(f32[2,1,1,12,128]{4,2,3,1,0:T(1,128)S(1)} %get-tuple-element.12), channel_id=1, source_target_pairs={{1,0},{2,1},{3,2},{4,3},{5,4},{6,5},{7,6},{9,8},{10,9},{11,10},{12... | collective-permute-start | bytes 36872 | tf_op jit(solution)/shard_map/ppermute | solution.py:21
  33.6 0.8 copy-start.1
  33.6 0.8 copy-start.4
  33.6 0.8 copy-start.5
  34.5 0.6 copy-start.3
  34.5 16.5 %copy-start.2 = (f32[1,8,12,128]{3,1,2,0:T(8,128)}, f32[1,8,12,128]{3,1,2,0:T(8,128)S(1)}, u32[]{:S(2)}) copy-start(f32[1,8,12,128]{3,1,2,0:T(8,128)S(1)} %get-tuple-element.7) | copy-start | bytes 147460
  43.8 18.5 %all-to-all-start = ((f32[96,1,128]{2,1,0:T(1,128)}), f32[96,1,128]{2,1,0:T(1,128)S(1)}, u32[]{:S(2)}, u32[]{:S(2)}) async-start(f32[96,1,128]{2,1,0:T(1,128)} %reshape.227), calls=%async_computation | async-start | bytes 98304 | tf_op jit(solution)/shard_map/all_to_all | solution.py:65
  62.3 22.3 %all-to-all-start.1 = ((f32[96,1,128]{2,1,0:T(1,128)}), f32[96,1,128]{2,1,0:T(1,128)S(1)}, u32[]{:S(2)}, u32[]{:S(2)}) async-start(f32[96,1,128]{2,1,0:T(1,128)} %reshape.225), calls=%async_computation.1 | async-start | bytes 98304 | tf_op jit(solution)/shard_map/all_to_all | solution.py:66
where the time goes:
time: 88.8 us; the launch traced here: 88.3 us
  starting transfers between devices  44.6 us (50%)
  other arithmetic  18.2 us (20%)
  waiting for transfers between devices  16.5 us (19%)
  local copies, waits for them, and re-layouts  7.67 us (9%)
  between operations  0.9 us (1%)
    ppermute x2, starting transfers between devices, shifted(): return lax.ppermute(value, axis, pairs)  19.6 us
    unnamed x2, other arithmetic  14.3 us
    all_to_all x1, starting transfers between devices, shards(): lax.all_to_all(flat_adjoint, 'tm', split_axis=2, concat_axis=0, tiled=True)  10.9 us
    all_to_all x1, waiting for transfers between devices, shards(): lax.all_to_all(flat_adjoint, 'tm', split_axis=2, concat_axis=0, tiled=True)  8.62 us
    all_to_all x1, starting transfers between devices, shards(): lax.all_to_all(flat_state, 'tm', split_axis=2, concat_axis=0, tiled=True)  6.85 us
    unnamed x17, local copies, waits for them, and re-layouts  6.11 us
    ppermute x1, starting transfers between devices, padded(): before = lax.ppermute(last, axis, up)  5.37 us
    ppermute x1, waiting for transfers between devices, padded(): after = lax.ppermute(leading, axis, down)  4.98 us
  transfers between devices with their start and end apart: 6, of which 3 were waited for; matrix products, arithmetic and copies ran while one was open for 14% of the time, Pallas kernels for 0%

commit v1 on v0

v1 whole, which is shorter than its diff:
```python
import functools
import math

import jax
import jax.numpy as jnp
import numpy as np
from jax import lax
from jax.experimental import pallas as pl
from jax.experimental.pallas import tpu as pltpu
from jax.sharding import PartitionSpec as P

diffusion = 0.05
control_cost = 0.2
tracking = 0.5

STEPS = 96
ROWS = 12
OWNERS = 8
BLOCK = 16
LANES = 128


def dft_table():
    times = np.arange(STEPS)
    angles = (np.outer(times, times) % STEPS) * (2.0 * math.pi / STEPS)
    table = np.zeros((OWNERS, ROWS, 2, 4, LANES))
    for r in range(OWNERS):
        for j in range(ROWS):
            for field in range(2):
                table[r, j, field, 2 * field, :STEPS] = np.cos(angles[8 * j + r])
                table[r, j, field, 2 * field + 1, :STEPS] = -np.sin(angles[8 * j + r])
    table = table.reshape(2 * STEPS, 4 * LANES) / math.sqrt(STEPS)
    trig = np.zeros((8, LANES))
    trig[0, :STEPS] = np.cos(times * (2.0 * math.pi / STEPS))
    trig[1, :STEPS] = np.sin(times * (2.0 * math.pi / STEPS))
    return table.astype(np.float32), trig.astype(np.float32)


def swap_blocks(tile):
    row = lax.broadcasted_iota(jnp.int32, (8, LANES), 0)
    block = lax.broadcasted_iota(jnp.int32, (8, LANES), 1) // BLOCK
    for bit in (1, 2, 4):
        row_set = (row & bit) != 0
        block_set = (block & bit) != 0
        up = pltpu.roll(pltpu.roll(tile, 8 - bit, 0), BLOCK * bit, 1)
        if bit == 4:
            tile = jnp.where(row_set == block_set, tile, up)
        else:
            down = pltpu.roll(pltpu.roll(tile, bit, 0), LANES - BLOCK * bit, 1)
            tile = jnp.where(row_set == block_set, tile, jnp.where(block_set, up, down))
    return tile


def kernel(
    s_hbm, p_hbm, target_hbm, cond_hbm, table_hbm, trig_ref,
    rs_ref, rp_ref, spec_ref,
    s_pad, p_v, w_pad, target_v, cond_v, table_v,
    s_prev, p_next, edge_low, edge_high, from_low, from_high,
    send_a, recv_a, send_b, recv_b, cond_rows,
    load_sem, near_send, near_recv, a_send, a_recv, b_send, b_recv,
):
    tm = lax.axis_index("tm")
    space = lax.axis_index("space")
    group = lax.div(tm, OWNERS)
    rank = lax.rem(tm, OWNERS)
    later = lax.rem(tm + 1, STEPS)
    earlier = lax.rem(tm + STEPS - 1, STEPS)
    above = lax.rem(space + 1, 8)
    below = lax.rem(space + 7, 8)

    loads = [
        pltpu.make_async_copy(source, target, load_sem.at[i])
        for i, (source, target) in enumerate(
            (
                (s_hbm, s_pad.at[pl.ds(1, ROWS)]),
                (p_hbm, p_v),
                (cond_hbm, cond_v),
                (target_hbm, target_v),
                (table_hbm, table_v),
            )
        )
    ]
    for load in loads:
        load.start()

    barrier = pltpu.get_barrier_semaphore()
    a_peers = [lax.rem(group + k, ROWS) for k in range(1, ROWS)]
    b_peers = [lax.rem(rank + k, OWNERS) for k in range(1, OWNERS)]
    for where in (
        [{"tm": later}, {"tm": earlier}, {"space": above}, {"space": below}]
        + [{"tm": peer * OWNERS + rank} for peer in a_peers]
        + [{"tm": group * OWNERS + peer} for peer in b_peers]
    ):
        pl.semaphore_signal(barrier, 1, device_id=where, device_id_type=pl.DeviceIdType.MESH)

    zero = jnp.zeros((8, LANES), jnp.float32)
    for padded in (s_pad, w_pad):
        padded[0] = zero
        padded[ROWS + 1] = zero
    for load in loads[:3]:
        load.wait()
    for x in range(ROWS):
        w_pad[x + 1] = cond_v[x] * p_v[x]
    for edge, z in ((edge_low, 0), (edge_high, 7)):
        edge[0:ROWS] = s_pad[1 : ROWS + 1, z, :]
        edge[ROWS : 2 * ROWS] = w_pad[1 : ROWS + 1, z, :]

    pl.semaphore_wait(barrier, 4 + ROWS - 1 + OWNERS - 1)

    def send(source, target, send_sem, recv_sem, where):
        copy = pltpu.make_async_remote_copy(
            src_ref=source, dst_ref=target, send_sem=send_sem, recv_sem=recv_sem,
            device_id=where, device_id_type=pl.DeviceIdType.MESH,
        )
        copy.start()
        return copy

    near = [
        send(s_pad.at[pl.ds(1, ROWS)], s_prev, near_send.at[0], near_recv.at[0], {"tm": later}),
        send(p_v, p_next, near_send.at[1], near_recv.at[1], {"tm": earlier}),
        send(edge_low, from_high, near_send.at[2], near_recv.at[2], {"space": below}),
        send(edge_high, from_low, near_send.at[3], near_recv.at[3], {"space": above}),
    ]

    cond_rows[...] = swap_blocks(cond_v[group])
    own_cond = jnp.broadcast_to(cond_rows[pl.ds(rank, 1)], (LANES, LANES)).T

    row = lax.broadcasted_iota(jnp.int32, (8, LANES), 0)
    lane = lax.broadcasted_iota(jnp.int32, (8, LANES), 1)
    loads[3].wait()
    for copy in near:
        copy.wait_recv()

    def around(padded, x, low, high):
        centre = padded[x + 1]
        low = jnp.broadcast_to(jnp.where(space == 0, 0.0, low), (8, LANES))
        high = jnp.broadcast_to(jnp.where(space == 7, 0.0, high), (8, LANES))
        z_low = jnp.where(row == 0, low, pltpu.roll(centre, 1, 0))
        z_high = jnp.where(row == 7, high, pltpu.roll(centre, 7, 0))
        y_low = jnp.where(lane == 0, 0.0, pltpu.roll(centre, 1, 1))
        y_high = jnp.where(lane == LANES - 1, 0.0, pltpu.roll(centre, LANES - 1, 1))
        return (z_low + z_high) + (padded[x] + padded[x + 2]) + (y_low + y_high)

    for x in range(ROWS):
        s, p, w, cond = s_pad[x + 1], p_v[x], w_pad[x + 1], cond_v[x]
        around_s = around(s_pad, x, from_low[x : x + 1], from_high[x : x + 1])
        around_w = around(
            w_pad, x, from_low[ROWS + x : ROWS + x + 1], from_high[ROWS + x : ROWS + x + 1]
        )
        rs = s - s_prev[x] + diffusion * (cond * (6.0 * s - around_s)) - control_cost * p
        rp = p - p_next[x] + diffusion * (6.0 * w - around_w) + tracking * (s - target_v[x])
        rs_ref[x] = rs
        rp_ref[x] = rp
        send_a[x, 0] = swap_blocks(rs)
        send_a[x, 1] = swap_blocks(rp)

    copies_a = [
        send(send_a.at[peer], recv_a.at[group], a_send.at[k], a_recv.at[k],
             {"tm": peer * OWNERS + rank})
        for k, peer in enumerate(a_peers)
    ]
    recv_a[group] = send_a[group]
    for copy in copies_a:
        copy.wait_recv()
    for block in range(OWNERS):
        for part in range(3):
            send_b[block, 8 * part : 8 * part + 8] = recv_a[
                4 * part : 4 * part + 4, :, block, :
            ].reshape(8, LANES)
    copies_b = [
        send(send_b.at[peer], recv_b.at[rank], b_send.at[k], b_recv.at[k],
             {"tm": group * OWNERS + peer})
        for k, peer in enumerate(b_peers)
    ]
    recv_b[rank] = send_b[rank]
    loads[4].wait()
    for copy in copies_b:
        copy.wait_recv()

    spectra = lax.dot_general(
        recv_b[...].reshape(2 * STEPS, LANES), table_v[...], (((0,), (0,)), ((), ())),
        precision=lax.Precision.HIGHEST, preferred_element_type=jnp.float32,
    )
    state_real, state_imag, adjoint_real, adjoint_imag = (
        spectra[:, LANES * i : LANES * (i + 1)] for i in range(4)
    )
    cosine, sine = trig_ref[0:1], trig_ref[1:2]
    diagonal = 1.0 + diffusion * 6.0 * own_cond - cosine
    scale = 1.0 / (diagonal * diagonal + sine * sine + control_cost * tracking)
    fixes = (
        diagonal * state_real + sine * state_imag + control_cost * adjoint_real,
        diagonal * state_imag - sine * state_real + control_cost * adjoint_imag,
        diagonal * adjoint_real - sine * adjoint_imag - tracking * state_real,
        diagonal * adjoint_imag + sine * adjoint_real - tracking * state_imag,
    )
    for i, fix in enumerate(fixes):
        spec_ref[i] = (fix * scale)[:, :STEPS]
    for copy in near + copies_a + copies_b:
        copy.wait_send()


def shards(state_field, adjoint, target, conductivity):
    table, trig = dft_table()
    tiles = (ROWS, 8, LANES)
    rows_first = lambda field: jnp.transpose(field[0], (1, 0, 2))
    vmem, dma = pltpu.VMEM, pltpu.SemaphoreType.DMA
    f32 = jnp.float32
    anywhere = pl.BlockSpec(memory_space=pl.ANY)
    in_vmem = pl.BlockSpec(memory_space=pltpu.VMEM)
    rs, rp, spec = pl.pallas_call(
        kernel,
        out_shape=(
            jax.ShapeDtypeStruct(tiles, f32),
            jax.ShapeDtypeStruct(tiles, f32),
            jax.ShapeDtypeStruct((4, LANES, STEPS), f32),
        ),
        in_specs=[anywhere] * 5 + [in_vmem],
        out_specs=(in_vmem,) * 3,
        scratch_shapes=[
            vmem((ROWS + 2, 8, LANES), f32),
            vmem(tiles, f32),
            vmem((ROWS + 2, 8, LANES), f32),
            vmem(tiles, f32),
            vmem(tiles, f32),
            vmem((2 * STEPS, 4 * LANES), f32),
            vmem(tiles, f32),
            vmem(tiles, f32),
            vmem((2 * ROWS, LANES), f32),
            vmem((2 * ROWS, LANES), f32),
            vmem((2 * ROWS, LANES), f32),
            vmem((2 * ROWS, LANES), f32),
            vmem((ROWS, 2, 8, LANES), f32),
            vmem((ROWS, 2, 8, LANES), f32),
            vmem((OWNERS, 2 * ROWS, LANES), f32),
            vmem((OWNERS, 2 * ROWS, LANES), f32),
            vmem((8, LANES), f32),
            dma((5,)),
            dma((4,)),
            dma((4,)),
            dma((ROWS - 1,)),
            dma((ROWS - 1,)),
            dma((OWNERS - 1,)),
            dma((OWNERS - 1,)),
        ],
        compiler_params=pltpu.CompilerParams(
            collective_id=0, has_side_effects=True, vmem_limit_bytes=24 * 1024 * 1024
        ),
    )(
        rows_first(state_field), rows_first(adjoint), rows_first(target),
        jnp.transpose(conductivity, (1, 0, 2)), jnp.asarray(table), jnp.asarray(trig),
    )
    back = lambda tile: jnp.transpose(tile, (1, 0, 2))[None]
    spectral = jnp.transpose(spec.reshape(4, 8, BLOCK, STEPS), (0, 3, 1, 2))
    return back(rs), back(rp), spectral


def solution(mesh):
    placed = (
        P("tm", "space", None, None),
        P("tm", "space", None, None),
        P("tm", "space", None, None),
        P("space", None, None),
    )
    return jax.shard_map(
        shards,
        mesh=mesh,
        in_specs=placed,
        out_specs=(
            P("tm", "space", None, None),
            P("tm", "space", None, None),
            P(None, None, "space", "tm"),
        ),
        check_vma=False,
    )
```

time: 88.8 us -> 43 us (0.48)
  the two profiles are of different devices: /device:TPU:17 before, /device:TPU:1 now
where the time goes in v1:
time: 43 us; the launch traced here: 42.6 us
  Pallas kernels  35.1 us (82%)
  local copies, waits for them, and re-layouts  6.81 us (16%)
  between operations  0.65 us (2%)
    pallas_call x1, Pallas kernels, shards(): pl.pallas_call(kernel, out_shape=(jax.ShapeDtypeStruct(tiles, f32), jax.S...  35.1 us
    unnamed x15, local copies, waits for them, and re-layouts  6.81 us

profile of v1, /device:TPU:1, one launch (start us, length us, event | category | flops | bytes accessed | tf_op | source)
XLA Modules:
  0.0 42.6 jit_solution(12499002146517362806)
XLA Ops:
  0.6 0.0 copy-start.5
  0.6 0.7 %copy-done.5 = f32[8,128]{1,0:T(8,128)S(1)} copy-done((f32[8,128]{1,0:T(8,128)S(1)}, f32[8,128]{1,0:T(8,128)}, u32[]{:S(2)}) %copy-start.5) | copy-done | bytes 4120
  1.3 0.0 copy-start
  1.3 1.0 %copy-done = f32[192,512]{1,0:T(8,128)S(1)} copy-done((f32[192,512]{1,0:T(8,128)S(1)}, f32[192,512]{1,0:T(8,128)}, u32[]{:S(2)}) %copy-start) | copy-done | bytes 393240
  2.3 0.0 copy-start.1
  2.3 0.8 %copy-done.1 = f32[1,8,12,128]{3,1,2,0:T(8,128)S(1)} copy-done((f32[1,8,12,128]{3,1,2,0:T(8,128)S(1)}, f32[1,8,12,128]{3,1,2,0:T(8,128)}, u32[]{:S(2)}) %copy-start.1) | copy-done | bytes 49176
  3.1 0.0 copy-start.2
  3.1 0.8 %copy-done.2 = f32[1,8,12,128]{3,1,2,0:T(8,128)S(1)} copy-done((f32[1,8,12,128]{3,1,2,0:T(8,128)S(1)}, f32[1,8,12,128]{3,1,2,0:T(8,128)}, u32[]{:S(2)}) %copy-start.2) | copy-done | bytes 49176
  3.9 0.0 copy-start.3
  3.9 0.8 %copy-done.3 = f32[1,8,12,128]{3,1,2,0:T(8,128)S(1)} copy-done((f32[1,8,12,128]{3,1,2,0:T(8,128)S(1)}, f32[1,8,12,128]{3,1,2,0:T(8,128)}, u32[]{:S(2)}) %copy-start.3) | copy-done | bytes 49176
  4.7 0.0 copy-start.4
  4.7 0.8 %copy-done.4 = f32[8,12,128]{2,0,1:T(8,128)S(1)} copy-done((f32[8,12,128]{2,0,1:T(8,128)S(1)}, f32[8,12,128]{2,0,1:T(8,128)}, u32[]{:S(2)}) %copy-start.4) | copy-done | bytes 49176
  5.5 35.1 %shard_map.85 = (f32[12,8,128]{2,1,0:T(8,128)S(1)}, f32[12,8,128]{2,1,0:T(8,128)S(1)}, f32[4,128,96]{2,1,0:T(8,128)S(1)}) custom-call(f32[12,8,128]{2,1,0:T(8,128)S(1)} %bitcast.20, f32[12,8,128]{2,1,0:T(8,128)S(1)} %bitcast.21, f32[12,8,128]{2,1,0:T(8,128)S(1)} %bitcast.22, f32[12,8,128]{2,1,0:T(8,128)S(1)} %bitcast.23, f32[192,512]{1,0:T(8,128)S(1)} %copy-done, ...), custom_call_target="tpu_custom_call" | custom-call | tf_op jit(solution)/shard_map/pallas_call | solution.py:210
  40.7 0.6 %copy.12 = f32[1,8,12,128]{3,1,2,0:T(8,128)} copy(f32[1,8,12,128]{3,1,2,0:T(8,128)S(1)} %bitcast.25) | data formatting | bytes 98304
  41.3 0.6 %copy.13 = f32[1,8,12,128]{3,1,2,0:T(8,128)} copy(f32[1,8,12,128]{3,1,2,0:T(8,128)S(1)} %bitcast.24) | data formatting | bytes 98304
  41.9 0.7 %copy.14 = f32[4,96,8,16]{1,3,2,0:T(8,128)} copy(f32[4,96,8,16]{1,3,2,0:T(8,128)S(1)} %bitcast.19) | data formatting | bytes 393216
Async XLA Ops:
  0.6 0.7 %copy-start.5 = (f32[8,128]{1,0:T(8,128)S(1)}, f32[8,128]{1,0:T(8,128)}, u32[]{:S(2)}) copy-start(f32[8,128]{1,0:T(8,128)} %constant.5.clone.trig_ref) | copy-start | bytes 12292
  1.3 1.0 %copy-start = (f32[192,512]{1,0:T(8,128)S(1)}, f32[192,512]{1,0:T(8,128)}, u32[]{:S(2)}) copy-start(f32[192,512]{1,0:T(8,128)} %constant.4.clone.table_hbm) | copy-start | bytes 1179652
  2.3 0.8 %copy-start.1 = (f32[1,8,12,128]{3,1,2,0:T(8,128)S(1)}, f32[1,8,12,128]{3,1,2,0:T(8,128)}, u32[]{:S(2)}) copy-start(f32[1,8,12,128]{3,1,2,0:T(8,128)} %param.6) | copy-start | bytes 147460
  3.1 0.8 %copy-start.2 = (f32[1,8,12,128]{3,1,2,0:T(8,128)S(1)}, f32[1,8,12,128]{3,1,2,0:T(8,128)}, u32[]{:S(2)}) copy-start(f32[1,8,12,128]{3,1,2,0:T(8,128)} %param.7) | copy-start | bytes 147460
  3.9 0.8 %copy-start.3 = (f32[1,8,12,128]{3,1,2,0:T(8,128)S(1)}, f32[1,8,12,128]{3,1,2,0:T(8,128)}, u32[]{:S(2)}) copy-start(f32[1,8,12,128]{3,1,2,0:T(8,128)} %param.8) | copy-start | bytes 147460
  4.7 0.8 %copy-start.4 = (f32[8,12,128]{2,0,1:T(8,128)S(1)}, f32[8,12,128]{2,0,1:T(8,128)}, u32[]{:S(2)}) copy-start(f32[8,12,128]{2,0,1:T(8,128)} %param.9) | copy-start | bytes 147460

commit v2 on v1

--- a/solution.py
+++ b/solution.py
@@ -17,6 +17,7 @@
 ROWS = 12
 OWNERS = 8
 BLOCK = 16
+TERMS = 2 * STEPS
 LANES = 128
 
 
@@ -33,7 +34,9 @@
     trig = np.zeros((8, LANES))
     trig[0, :STEPS] = np.cos(times * (2.0 * math.pi / STEPS))
     trig[1, :STEPS] = np.sin(times * (2.0 * math.pi / STEPS))
-    return table.astype(np.float32), trig.astype(np.float32)
+    rows = np.zeros((8, 4 * LANES))
+    rows[:, :LANES] = trig
+    return np.concatenate([table, rows]).astype(np.float32)
 
 
 def swap_blocks(tile):
@@ -52,11 +55,11 @@
 
 
 def kernel(
-    s_hbm, p_hbm, target_hbm, cond_hbm, table_hbm, trig_ref,
-    rs_ref, rp_ref, spec_ref,
-    s_pad, p_v, w_pad, target_v, cond_v, table_v,
+    s_hbm, p_hbm, target_hbm, cond_hbm, table_hbm,
+    rs_ref, rp_ref, recv_b, own_cond, table_v,
+    s_pad, p_v, w_pad, target_v, cond_v,
     s_prev, p_next, edge_low, edge_high, from_low, from_high,
-    send_a, recv_a, send_b, recv_b, cond_rows,
+    send_a, recv_a, send_b, cond_rows,
     load_sem, near_send, near_recv, a_send, a_recv, b_send, b_recv,
 ):
     tm = lax.axis_index("tm")
@@ -123,7 +126,7 @@
     ]
 
     cond_rows[...] = swap_blocks(cond_v[group])
-    own_cond = jnp.broadcast_to(cond_rows[pl.ds(rank, 1)], (LANES, LANES)).T
+    own_cond[...] = jnp.broadcast_to(cond_rows[pl.ds(rank, 1)], (LANES, LANES)).T
 
     row = lax.broadcasted_iota(jnp.int32, (8, LANES), 0)
     lane = lax.broadcasted_iota(jnp.int32, (8, LANES), 1)
@@ -177,15 +180,30 @@
     for copy in copies_b:
         copy.wait_recv()
 
+    for copy in near + copies_a + copies_b:
+        copy.wait_send()
+
+
+def solve(
+    rs_ref, rp_ref, recv_b, own_cond, table_v,
+    rs_hbm, rp_hbm, spec_hbm,
+    spec_v, sem,
+):
+    copies = [
+        pltpu.make_async_copy(rs_ref, rs_hbm, sem.at[0]),
+        pltpu.make_async_copy(rp_ref, rp_hbm, sem.at[1]),
+    ]
+    for copy in copies:
+        copy.start()
     spectra = lax.dot_general(
-        recv_b[...].reshape(2 * STEPS, LANES), table_v[...], (((0,), (0,)), ((), ())),
+        recv_b[...].reshape(2 * STEPS, LANES), table_v[0:TERMS], (((0,), (0,)), ((), ())),
         precision=lax.Precision.HIGHEST, preferred_element_type=jnp.float32,
     )
     state_real, state_imag, adjoint_real, adjoint_imag = (
         spectra[:, LANES * i : LANES * (i + 1)] for i in range(4)
     )
-    cosine, sine = trig_ref[0:1], trig_ref[1:2]
-    diagonal = 1.0 + diffusion * 6.0 * own_cond - cosine
+    cosine, sine = table_v[TERMS : TERMS + 1, :LANES], table_v[TERMS + 1 : TERMS + 2, :LANES]
+    diagonal = 1.0 + diffusion * 6.0 * own_cond[...] - cosine
     scale = 1.0 / (diagonal * diagonal + sine * sine + control_cost * tracking)
     fixes = (
         diagonal * state_real + sine * state_imag + control_cost * adjoint_real,
@@ -194,35 +212,40 @@
         diagonal * adjoint_imag + sine * adjoint_real - tracking * state_imag,
     )
     for i, fix in enumerate(fixes):
-        spec_ref[i] = (fix * scale)[:, :STEPS]
-    for copy in near + copies_a + copies_b:
-        copy.wait_send()
+        spec_v[i] = (fix * scale)[:, :STEPS]
+        copy = pltpu.make_async_copy(spec_v.at[i], spec_hbm.at[i], sem.at[2 + i])
+        copy.start()
+        copies.append(copy)
+    for copy in copies:
+        copy.wait()
 
 
 def shards(state_field, adjoint, target, conductivity):
-    table, trig = dft_table()
+    table = dft_table()
     tiles = (ROWS, 8, LANES)
-    rows_first = lambda field: jnp.transpose(field[0], (1, 0, 2))
+    stay = lambda array: pltpu.with_memory_space_constraint(array, pltpu.HBM)
+    rows_first = lambda field: stay(jnp.transpose(field[0], (1, 0, 2)))
     vmem, dma = pltpu.VMEM, pltpu.SemaphoreType.DMA
     f32 = jnp.float32
-    anywhere = pl.BlockSpec(memory_space=pl.ANY)
+    in_hbm = pl.BlockSpec(memory_space=pltpu.HBM)
     in_vmem = pl.BlockSpec(memory_space=pltpu.VMEM)
-    rs, rp, spec = pl.pallas_call(
+    rs, rp, got, own_cond, table = pl.pallas_call(
         kernel,
         out_shape=(
             jax.ShapeDtypeStruct(tiles, f32),
             jax.ShapeDtypeStruct(tiles, f32),
-            jax.ShapeDtypeStruct((4, LANES, STEPS), f32),
+            jax.ShapeDtypeStruct((OWNERS, 2 * ROWS, LANES), f32),
+            jax.ShapeDtypeStruct((LANES, LANES), f32),
+            jax.ShapeDtypeStruct((TERMS + 8, 4 * LANES), f32),
         ),
-        in_specs=[anywhere] * 5 + [in_vmem],
-        out_specs=(in_vmem,) * 3,
+        in_specs=[in_hbm] * 5,
+        out_specs=(in_vmem,) * 5,
         scratch_shapes=[
             vmem((ROWS + 2, 8, LANES), f32),
             vmem(tiles, f32),
             vmem((ROWS + 2, 8, LANES), f32),
             vmem(tiles, f32),
             vmem(tiles, f32),
-            vmem((2 * STEPS, 4 * LANES), f32),
             vmem(tiles, f32),
             vmem(tiles, f32),
             vmem((2 * ROWS, LANES), f32),
@@ -231,7 +254,6 @@
             vmem((2 * ROWS, LANES), f32),
             vmem((ROWS, 2, 8, LANES), f32),
             vmem((ROWS, 2, 8, LANES), f32),
-            vmem((OWNERS, 2 * ROWS, LANES), f32),
             vmem((OWNERS, 2 * ROWS, LANES), f32),
             vmem((8, LANES), f32),
             dma((5,)),
@@ -247,8 +269,20 @@
         ),
     )(
         rows_first(state_field), rows_first(adjoint), rows_first(target),
-        jnp.transpose(conductivity, (1, 0, 2)), jnp.asarray(table), jnp.asarray(trig),
-    )
+        stay(jnp.transpose(conductivity, (1, 0, 2))), stay(jnp.asarray(table)),
+    )
+    rs, rp, spec = pl.pallas_call(
+        solve,
+        out_shape=(
+            jax.ShapeDtypeStruct(tiles, f32),
+            jax.ShapeDtypeStruct(tiles, f32),
+            jax.ShapeDtypeStruct((4, LANES, STEPS), f32),
+        ),
+        in_specs=[in_vmem] * 5,
+        out_specs=(in_hbm,) * 3,
+        scratch_shapes=[vmem((4, LANES, STEPS), f32), dma((6,))],
+        compiler_params=pltpu.CompilerParams(vmem_limit_bytes=16 * 1024 * 1024),
+    )(rs, rp, got, own_cond, table)
     back = lambda tile: jnp.transpose(tile, (1, 0, 2))[None]
     spectral = jnp.transpose(spec.reshape(4, 8, BLOCK, STEPS), (0, 3, 1, 2))
     return back(rs), back(rp), spectral

time: 43 us -> 36.2 us (0.84)
  local copies, waits for them, and re-layouts: 6.81 us -> 0 us
    unnamed x15 -> x0, local copies, waits for them, and re-layouts: 6.81 us -> none
    pallas_call x0 -> x1, Pallas kernels: none -> 1.19 us  [shards(): pl.pallas_call(solve, out_shape=(jax.ShapeDtypeStruct(tiles, f32), jax.Sh...]
    pallas_call x1, Pallas kernels: 35.1 us -> 34.3 us  [shards(): pl.pallas_call(kernel, out_shape=(jax.ShapeDtypeStruct(tiles, f32), jax.S...]
where the time goes in v2:
time: 36.2 us; the launch traced here: 36.1 us
  Pallas kernels  35.5 us (98%)
  between operations  0.64 us (2%)
    pallas_call x1, Pallas kernels, shards(): pl.pallas_call(kernel, out_shape=(jax.ShapeDtypeStruct(tiles, f32), jax.S...  34.3 us
    pallas_call x1, Pallas kernels, shards(): pl.pallas_call(solve, out_shape=(jax.ShapeDtypeStruct(tiles, f32), jax.Sh...  1.19 us

profile of v2, /device:TPU:1, one launch (start us, length us, event | category | flops | bytes accessed | tf_op | source)
XLA Modules:
  0.0 36.1 jit_solution(12553575896910267898)
XLA Ops:
  0.6 34.3 %shard_map.76 = (f32[12,8,128]{2,1,0:T(8,128)S(1)}, f32[12,8,128]{2,1,0:T(8,128)S(1)}, f32[8,24,128]{2,1,0:T(8,128)S(1)}, f32[128,128]{1,0:T(8,128)S(1)}, f32[200,512]{1,0:T(8,128)S(1)}) custom-call(f32[12,8,128]{2,1,0:T(8,128)} %bitcast.19, f32[12,8,128]{2,1,0:T(8,128)} %bitcast.20, f32[12,8,128]{2,1,0:T(8,128)} %bitcast.21, f32[12,8,128]{2,1,0:T(8,128)} %bitcast.22, ...), custom_call_target="tpu_custom_call" | custom-call | tf_op jit(solution)/shard_map/pallas_call | solution.py:232
  34.9 1.2 %shard_map.77 = (f32[12,8,128]{2,1,0:T(8,128)}, f32[12,8,128]{2,1,0:T(8,128)}, f32[4,128,96]{2,1,0:T(8,128)}) custom-call(f32[12,8,128]{2,1,0:T(8,128)S(1)} %get-tuple-element.11.rs_ref, f32[12,8,128]{2,1,0:T(8,128)S(1)} %get-tuple-element.12.rp_ref, f32[8,24,128]{2,1,0:T(8,128)S(1)} %get-tuple-element.13.recv_b, f32[128,128]{1,0:T(8,128)S(1)} %get-tuple-element.14.own_cond, ...), custom_call_target="tpu_custom_call" | custom-call | tf_op jit(solution)/shard_map/pallas_call | solution.py:274

commit v3 on v2

--- a/solution.py
+++ b/solution.py
@@ -14,6 +14,7 @@
 tracking = 0.5
 
 STEPS = 96
+DEPTH = 12
 ROWS = 12
 OWNERS = 8
 BLOCK = 16
@@ -24,12 +25,10 @@
 def dft_table():
     times = np.arange(STEPS)
     angles = (np.outer(times, times) % STEPS) * (2.0 * math.pi / STEPS)
-    table = np.zeros((OWNERS, ROWS, 2, 4, LANES))
-    for r in range(OWNERS):
-        for j in range(ROWS):
-            for field in range(2):
-                table[r, j, field, 2 * field, :STEPS] = np.cos(angles[8 * j + r])
-                table[r, j, field, 2 * field + 1, :STEPS] = -np.sin(angles[8 * j + r])
+    table = np.zeros((STEPS, 2, 4, LANES))
+    for field in range(2):
+        table[:, field, 2 * field, :STEPS] = np.cos(angles)
+        table[:, field, 2 * field + 1, :STEPS] = -np.sin(angles)
     table = table.reshape(2 * STEPS, 4 * LANES) / math.sqrt(STEPS)
     trig = np.zeros((8, LANES))
     trig[0, :STEPS] = np.cos(times * (2.0 * math.pi / STEPS))
@@ -56,11 +55,11 @@
 
 def kernel(
     s_hbm, p_hbm, target_hbm, cond_hbm, table_hbm,
-    rs_ref, rp_ref, recv_b, own_cond, table_v,
+    rs_ref, rp_ref, got, own_cond, table_v,
     s_pad, p_v, w_pad, target_v, cond_v,
     s_prev, p_next, edge_low, edge_high, from_low, from_high,
-    send_a, recv_a, send_b, cond_rows,
-    load_sem, near_send, near_recv, a_send, a_recv, b_send, b_recv,
+    blocks, cond_rows,
+    load_sem, near_send, near_recv, block_send, block_recv,
 ):
     tm = lax.axis_index("tm")
     space = lax.axis_index("space")
@@ -87,14 +86,26 @@
         load.start()
 
     barrier = pltpu.get_barrier_semaphore()
-    a_peers = [lax.rem(group + k, ROWS) for k in range(1, ROWS)]
-    b_peers = [lax.rem(rank + k, OWNERS) for k in range(1, OWNERS)]
-    for where in (
-        [{"tm": later}, {"tm": earlier}, {"space": above}, {"space": below}]
-        + [{"tm": peer * OWNERS + rank} for peer in a_peers]
-        + [{"tm": group * OWNERS + peer} for peer in b_peers]
-    ):
+    for where in ({"space": above}, {"space": below}):
         pl.semaphore_signal(barrier, 1, device_id=where, device_id_type=pl.DeviceIdType.MESH)
+
+    x, y, z = lax.div(tm, 2 * DEPTH), lax.rem(tm, 2), lax.rem(lax.div(tm, 2), DEPTH)
+
+    def partner(i):
+        level = lax.div(i, 8)
+        away = 6 - lax.div(level + 1, 2)
+        away = away + lax.rem(level, 2) * (DEPTH - 2 * away)
+        to_x = lax.rem(x + lax.div(lax.rem(i, 8), 2) + 1, 4)
+        to_y = lax.rem(y + i + 1, 2)
+        return 2 * DEPTH * to_x + 2 * lax.rem(z + away, DEPTH) + to_y
+
+    def greet(i, carry):
+        pl.semaphore_signal(
+            barrier, 1, device_id={"tm": partner(i)}, device_id_type=pl.DeviceIdType.MESH
+        )
+        return carry
+
+    lax.fori_loop(0, STEPS - 1, greet, 0)
 
     zero = jnp.zeros((8, LANES), jnp.float32)
     for padded in (s_pad, w_pad):
@@ -102,13 +113,13 @@
         padded[ROWS + 1] = zero
     for load in loads[:3]:
         load.wait()
-    for x in range(ROWS):
-        w_pad[x + 1] = cond_v[x] * p_v[x]
-    for edge, z in ((edge_low, 0), (edge_high, 7)):
-        edge[0:ROWS] = s_pad[1 : ROWS + 1, z, :]
-        edge[ROWS : 2 * ROWS] = w_pad[1 : ROWS + 1, z, :]
-
-    pl.semaphore_wait(barrier, 4 + ROWS - 1 + OWNERS - 1)
+    for i in range(ROWS):
+        w_pad[i + 1] = cond_v[i] * p_v[i]
+    for edge, plane in ((edge_low, 0), (edge_high, 7)):
+        edge[0:ROWS] = s_pad[1 : ROWS + 1, plane, :]
+        edge[ROWS : 2 * ROWS] = w_pad[1 : ROWS + 1, plane, :]
+
+    pl.semaphore_wait(barrier, STEPS - 1 + 2)
 
     def send(source, target, send_sem, recv_sem, where):
         copy = pltpu.make_async_remote_copy(
@@ -134,58 +145,50 @@
     for copy in near:
         copy.wait_recv()
 
-    def around(padded, x, low, high):
-        centre = padded[x + 1]
+    def around(padded, i, low, high):
+        centre = padded[i + 1]
         low = jnp.broadcast_to(jnp.where(space == 0, 0.0, low), (8, LANES))
         high = jnp.broadcast_to(jnp.where(space == 7, 0.0, high), (8, LANES))
         z_low = jnp.where(row == 0, low, pltpu.roll(centre, 1, 0))
         z_high = jnp.where(row == 7, high, pltpu.roll(centre, 7, 0))
         y_low = jnp.where(lane == 0, 0.0, pltpu.roll(centre, 1, 1))
         y_high = jnp.where(lane == LANES - 1, 0.0, pltpu.roll(centre, LANES - 1, 1))
-        return (z_low + z_high) + (padded[x] + padded[x + 2]) + (y_low + y_high)
-
-    for x in range(ROWS):
-        s, p, w, cond = s_pad[x + 1], p_v[x], w_pad[x + 1], cond_v[x]
-        around_s = around(s_pad, x, from_low[x : x + 1], from_high[x : x + 1])
+        return (z_low + z_high) + (padded[i] + padded[i + 2]) + (y_low + y_high)
+
+    for i in range(ROWS):
+        s, p, w, cond = s_pad[i + 1], p_v[i], w_pad[i + 1], cond_v[i]
+        around_s = around(s_pad, i, from_low[i : i + 1], from_high[i : i + 1])
         around_w = around(
-            w_pad, x, from_low[ROWS + x : ROWS + x + 1], from_high[ROWS + x : ROWS + x + 1]
+            w_pad, i, from_low[ROWS + i : ROWS + i + 1], from_high[ROWS + i : ROWS + i + 1]
         )
-        rs = s - s_prev[x] + diffusion * (cond * (6.0 * s - around_s)) - control_cost * p
-        rp = p - p_next[x] + diffusion * (6.0 * w - around_w) + tracking * (s - target_v[x])
-        rs_ref[x] = rs
-        rp_ref[x] = rp
-        send_a[x, 0] = swap_blocks(rs)
-        send_a[x, 1] = swap_blocks(rp)
-
-    copies_a = [
-        send(send_a.at[peer], recv_a.at[group], a_send.at[k], a_recv.at[k],
-             {"tm": peer * OWNERS + rank})
-        for k, peer in enumerate(a_peers)
-    ]
-    recv_a[group] = send_a[group]
-    for copy in copies_a:
-        copy.wait_recv()
-    for block in range(OWNERS):
-        for part in range(3):
-            send_b[block, 8 * part : 8 * part + 8] = recv_a[
-                4 * part : 4 * part + 4, :, block, :
-            ].reshape(8, LANES)
-    copies_b = [
-        send(send_b.at[peer], recv_b.at[rank], b_send.at[k], b_recv.at[k],
-             {"tm": group * OWNERS + peer})
-        for k, peer in enumerate(b_peers)
-    ]
-    recv_b[rank] = send_b[rank]
+        rs = s - s_prev[i] + diffusion * (cond * (6.0 * s - around_s)) - control_cost * p
+        rp = p - p_next[i] + diffusion * (6.0 * w - around_w) + tracking * (s - target_v[i])
+        rs_ref[i] = rs
+        rp_ref[i] = rp
+        blocks[pl.ds(16 * i, 8, stride=2)] = swap_blocks(rs)
+        blocks[pl.ds(16 * i + 1, 8, stride=2)] = swap_blocks(rp)
+
+    mine = pl.ds(pl.multiple_of(2 * tm, 2), 2)
+    own = pltpu.make_async_copy(blocks.at[mine], got.at[mine], block_recv)
+    own.start()
+
+    def hand_out(i, carry):
+        peer = partner(i)
+        theirs = pl.ds(pl.multiple_of(2 * peer, 2), 2)
+        send(blocks.at[theirs], got.at[mine], block_send, block_recv, {"tm": peer})
+        return carry
+
+    lax.fori_loop(0, STEPS - 1, hand_out, 0)
     loads[4].wait()
-    for copy in copies_b:
-        copy.wait_recv()
-
-    for copy in near + copies_a + copies_b:
+    pltpu.make_async_copy(got, got, block_recv).wait()
+    sent = blocks.at[pl.ds(0, TERMS - 2)]
+    pltpu.make_async_copy(sent, sent, block_send).wait()
+    for copy in near:
         copy.wait_send()
 
 
 def solve(
-    rs_ref, rp_ref, recv_b, own_cond, table_v,
+    rs_ref, rp_ref, got, own_cond, table_v,
     rs_hbm, rp_hbm, spec_hbm,
     spec_v, sem,
 ):
@@ -196,7 +199,7 @@
     for copy in copies:
         copy.start()
     spectra = lax.dot_general(
-        recv_b[...].reshape(2 * STEPS, LANES), table_v[0:TERMS], (((0,), (0,)), ((), ())),
+        got[...], table_v[0:TERMS], (((0,), (0,)), ((), ())),
         precision=lax.Precision.HIGHEST, preferred_element_type=jnp.float32,
     )
     state_real, state_imag, adjoint_real, adjoint_imag = (
@@ -234,7 +237,7 @@
         out_shape=(
             jax.ShapeDtypeStruct(tiles, f32),
             jax.ShapeDtypeStruct(tiles, f32),
-            jax.ShapeDtypeStruct((OWNERS, 2 * ROWS, LANES), f32),
+            jax.ShapeDtypeStruct((TERMS, LANES), f32),
             jax.ShapeDtypeStruct((LANES, LANES), f32),
             jax.ShapeDtypeStruct((TERMS + 8, 4 * LANES), f32),
         ),
@@ -252,17 +255,13 @@
             vmem((2 * ROWS, LANES), f32),
             vmem((2 * ROWS, LANES), f32),
             vmem((2 * ROWS, LANES), f32),
-            vmem((ROWS, 2, 8, LANES), f32),
-            vmem((ROWS, 2, 8, LANES), f32),
-            vmem((OWNERS, 2 * ROWS, LANES), f32),
+            vmem((TERMS, LANES), f32),
             vmem((8, LANES), f32),
             dma((5,)),
             dma((4,)),
             dma((4,)),
-            dma((ROWS - 1,)),
-            dma((ROWS - 1,)),
-            dma((OWNERS - 1,)),
-            dma((OWNERS - 1,)),
+            dma,
+            dma,
         ],
         compiler_params=pltpu.CompilerParams(
             collective_id=0, has_side_effects=True, vmem_limit_bytes=24 * 1024 * 1024

time: 36.2 us -> 34.8 us (0.961)
  Pallas kernels: 35.5 us -> 34 us
    pallas_call x1, Pallas kernels: 34.3 us -> 32.8 us  [shards(): pl.pallas_call(kernel, out_shape=(jax.ShapeDtypeStruct(tiles, f32), jax.S...]
where the time goes in v3:
time: 34.8 us; the launch traced here: 34.6 us
  Pallas kernels  34 us (98%)
  between operations  0.64 us (2%)
    pallas_call x1, Pallas kernels, shards(): pl.pallas_call(kernel, out_shape=(jax.ShapeDtypeStruct(tiles, f32), jax.S...  32.8 us
    pallas_call x1, Pallas kernels, shards(): pl.pallas_call(solve, out_shape=(jax.ShapeDtypeStruct(tiles, f32), jax.Sh...  1.19 us

profile of v3, /device:TPU:1, one launch (start us, length us, event | category | flops | bytes accessed | tf_op | source)
XLA Modules:
  0.0 34.6 jit_solution(1966752445882780438)
XLA Ops:
  0.6 32.8 %shard_map.76 = (f32[12,8,128]{2,1,0:T(8,128)S(1)}, f32[12,8,128]{2,1,0:T(8,128)S(1)}, f32[192,128]{1,0:T(8,128)S(1)}, f32[128,128]{1,0:T(8,128)S(1)}, f32[200,512]{1,0:T(8,128)S(1)}) custom-call(f32[12,8,128]{2,1,0:T(8,128)} %bitcast.19, f32[12,8,128]{2,1,0:T(8,128)} %bitcast.20, f32[12,8,128]{2,1,0:T(8,128)} %bitcast.21, f32[12,8,128]{2,1,0:T(8,128)} %bitcast.22, ...), custom_call_target="tpu_custom_call" | custom-call | tf_op jit(solution)/shard_map/pallas_call | solution.py:235
  33.4 1.2 %shard_map.77 = (f32[12,8,128]{2,1,0:T(8,128)}, f32[12,8,128]{2,1,0:T(8,128)}, f32[4,128,96]{2,1,0:T(8,128)}) custom-call(f32[12,8,128]{2,1,0:T(8,128)S(1)} %get-tuple-element.11.rs_ref, f32[12,8,128]{2,1,0:T(8,128)S(1)} %get-tuple-element.12.rp_ref, f32[192,128]{1,0:T(8,128)S(1)} %get-tuple-element.13.got, f32[128,128]{1,0:T(8,128)S(1)} %get-tuple-element.14.own_cond, ...), custom_call_target="tpu_custom_call" | custom-call | tf_op jit(solution)/shard_map/pallas_call | solution.py:273

commit v4 on v3

--- a/solution.py
+++ b/solution.py
@@ -59,7 +59,7 @@
     s_pad, p_v, w_pad, target_v, cond_v,
     s_prev, p_next, edge_low, edge_high, from_low, from_high,
     blocks, cond_rows,
-    load_sem, near_send, near_recv, block_send, block_recv,
+    load_sem, near_send, near_recv, block_send, block_recv, token, ready,
 ):
     tm = lax.axis_index("tm")
     space = lax.axis_index("space")
@@ -85,27 +85,29 @@
     for load in loads:
         load.start()
 
+    x, y, z = lax.div(tm, 2 * DEPTH), lax.rem(tm, 2), lax.rem(lax.div(tm, 2), DEPTH)
+
+    def at_plane(plane, j):
+        return 2 * DEPTH * lax.rem(x + j // 2, 4) + 2 * plane + lax.rem(y + j, 2)
+
+    def signal(semaphore, where):
+        pl.semaphore_signal(semaphore, 1, device_id=where, device_id_type=pl.DeviceIdType.MESH)
+
     barrier = pltpu.get_barrier_semaphore()
-    for where in ({"space": above}, {"space": below}):
-        pl.semaphore_signal(barrier, 1, device_id=where, device_id_type=pl.DeviceIdType.MESH)
-
-    x, y, z = lax.div(tm, 2 * DEPTH), lax.rem(tm, 2), lax.rem(lax.div(tm, 2), DEPTH)
-
-    def partner(i):
-        level = lax.div(i, 8)
-        away = 6 - lax.div(level + 1, 2)
-        away = away + lax.rem(level, 2) * (DEPTH - 2 * away)
-        to_x = lax.rem(x + lax.div(lax.rem(i, 8), 2) + 1, 4)
-        to_y = lax.rem(y + i + 1, 2)
-        return 2 * DEPTH * to_x + 2 * lax.rem(z + away, DEPTH) + to_y
-
-    def greet(i, carry):
-        pl.semaphore_signal(
-            barrier, 1, device_id={"tm": partner(i)}, device_id_type=pl.DeviceIdType.MESH
-        )
-        return carry
-
-    lax.fori_loop(0, STEPS - 1, greet, 0)
+    signal(barrier, {"space": above})
+    signal(barrier, {"space": below})
+    signal(barrier, {"tm": lax.rem(tm + STEPS - 1 + 2 * y, STEPS)})
+
+    @pl.when(z > 0)
+    def _():
+        signal(barrier, {"tm": tm - 2})
+
+    @pl.when(z < DEPTH - 1)
+    def _():
+        signal(barrier, {"tm": tm + 2})
+
+    for j in range(1, 8):
+        signal(barrier, {"tm": at_plane(z, j)})
 
     zero = jnp.zeros((8, LANES), jnp.float32)
     for padded in (s_pad, w_pad):
@@ -119,7 +121,7 @@
         edge[0:ROWS] = s_pad[1 : ROWS + 1, plane, :]
         edge[ROWS : 2 * ROWS] = w_pad[1 : ROWS + 1, plane, :]
 
-    pl.semaphore_wait(barrier, STEPS - 1 + 2)
+    pl.semaphore_wait(barrier, 10 + (z + 10) // (DEPTH - 1) + (21 - z) // (DEPTH - 1))
 
     def send(source, target, send_sem, recv_sem, where):
         copy = pltpu.make_async_remote_copy(
@@ -135,6 +137,23 @@
         send(edge_low, from_high, near_send.at[2], near_recv.at[2], {"space": below}),
         send(edge_high, from_low, near_send.at[3], near_recv.at[3], {"space": above}),
     ]
+
+    @pl.when(z > 0)
+    def _():
+        pl.semaphore_wait(token, 1)
+
+    @pl.when(z < DEPTH - 1)
+    def _():
+        @pl.when(y == 1)
+        def _():
+            signal(token, {"tm": tm + 2})
+            signal(token, {"tm": tm + 1})
+
+    def announce(plane, carry):
+        signal(ready, {"tm": at_plane(plane, 0)})
+        return carry
+
+    lax.fori_loop(0, z, announce, 0)
 
     cond_rows[...] = swap_blocks(cond_v[group])
     own_cond[...] = jnp.broadcast_to(cond_rows[pl.ds(rank, 1)], (LANES, LANES)).T
@@ -172,13 +191,24 @@
     own = pltpu.make_async_copy(blocks.at[mine], got.at[mine], block_recv)
     own.start()
 
-    def hand_out(i, carry):
-        peer = partner(i)
-        theirs = pl.ds(pl.multiple_of(2 * peer, 2), 2)
-        send(blocks.at[theirs], got.at[mine], block_send, block_recv, {"tm": peer})
+    def serve(plane, first):
+        for j in range(first, 8):
+            peer = at_plane(plane, j)
+            theirs = pl.ds(pl.multiple_of(2 * peer, 2), 2)
+            send(blocks.at[theirs], got.at[mine], block_send, block_recv, {"tm": peer})
+
+    def serve_plane(plane, carry):
+        serve(plane, 0)
         return carry
 
-    lax.fori_loop(0, STEPS - 1, hand_out, 0)
+    lax.fori_loop(0, z, serve_plane, 0)
+    serve(z, 1)
+
+    @pl.when(z < DEPTH - 1)
+    def _():
+        pl.semaphore_wait(ready, DEPTH - 1 - z)
+
+    lax.fori_loop(z + 1, DEPTH, serve_plane, 0)
     loads[4].wait()
     pltpu.make_async_copy(got, got, block_recv).wait()
     sent = blocks.at[pl.ds(0, TERMS - 2)]
@@ -262,6 +292,8 @@
             dma((4,)),
             dma,
             dma,
+            pltpu.SemaphoreType.REGULAR,
+            pltpu.SemaphoreType.REGULAR,
         ],
         compiler_params=pltpu.CompilerParams(
             collective_id=0, has_side_effects=True, vmem_limit_bytes=24 * 1024 * 1024

time: 34.8 us -> 32 us (0.920)
  the two profiles are of different devices: /device:TPU:1 before, /device:TPU:8 now
where the time goes in v4:
time: 32 us; the launch traced here: 31.9 us
  Pallas kernels  31.2 us (98%)
  between operations  0.64 us (2%)
    pallas_call x1, Pallas kernels, shards(): pl.pallas_call(kernel, out_shape=(jax.ShapeDtypeStruct(tiles, f32), jax.S...  30 us
    pallas_call x1, Pallas kernels, shards(): pl.pallas_call(solve, out_shape=(jax.ShapeDtypeStruct(tiles, f32), jax.Sh...  1.19 us

profile of v4, /device:TPU:8, one launch (start us, length us, event | category | flops | bytes accessed | tf_op | source)
XLA Modules:
  0.0 31.9 jit_solution(12652043002342812365)
XLA Ops:
  0.6 30.0 %shard_map.76 = (f32[12,8,128]{2,1,0:T(8,128)S(1)}, f32[12,8,128]{2,1,0:T(8,128)S(1)}, f32[192,128]{1,0:T(8,128)S(1)}, f32[128,128]{1,0:T(8,128)S(1)}, f32[200,512]{1,0:T(8,128)S(1)}) custom-call(f32[12,8,128]{2,1,0:T(8,128)} %bitcast.19, f32[12,8,128]{2,1,0:T(8,128)} %bitcast.20, f32[12,8,128]{2,1,0:T(8,128)} %bitcast.21, f32[12,8,128]{2,1,0:T(8,128)} %bitcast.22, ...), custom_call_target="tpu_custom_call" | custom-call | tf_op jit(solution)/shard_map/pallas_call | solution.py:265
  30.7 1.2 %shard_map.77 = (f32[12,8,128]{2,1,0:T(8,128)}, f32[12,8,128]{2,1,0:T(8,128)}, f32[4,128,96]{2,1,0:T(8,128)}) custom-call(f32[12,8,128]{2,1,0:T(8,128)S(1)} %get-tuple-element.11.rs_ref, f32[12,8,128]{2,1,0:T(8,128)S(1)} %get-tuple-element.12.rp_ref, f32[192,128]{1,0:T(8,128)S(1)} %get-tuple-element.13.got, f32[128,128]{1,0:T(8,128)S(1)} %get-tuple-element.14.own_cond, ...), custom_call_target="tpu_custom_call" | custom-call | tf_op jit(solution)/shard_map/pallas_call | solution.py:305

commit v5 on v4

v5 whole, which is shorter than its diff:
```python
import functools
import math

import jax
import jax.numpy as jnp
import numpy as np
from jax import lax
from jax.experimental import pallas as pl
from jax.experimental.pallas import tpu as pltpu
from jax.sharding import PartitionSpec as P

diffusion = 0.05
control_cost = 0.2
tracking = 0.5

STEPS = 96
DEPTH = 12
HALF = 8
ROWS = 12
OWNERS = 8
BLOCK = 16
TERMS = 2 * STEPS
LANES = 128


def dft_table():
    times = np.arange(STEPS)
    angles = (np.outer(times, times) % STEPS) * (2.0 * math.pi / STEPS)
    table = np.zeros((STEPS, 2, 4, LANES))
    for field in range(2):
        table[:, field, 2 * field, :STEPS] = np.cos(angles)
        table[:, field, 2 * field + 1, :STEPS] = -np.sin(angles)
    table = table.reshape(2 * STEPS, 4 * LANES) / math.sqrt(STEPS)
    trig = np.zeros((8, LANES))
    trig[0, :STEPS] = np.cos(times * (2.0 * math.pi / STEPS))
    trig[1, :STEPS] = np.sin(times * (2.0 * math.pi / STEPS))
    table = table.astype(np.float32)
    high = table.astype(jnp.bfloat16)
    return high, (table - high.astype(np.float32)).astype(jnp.bfloat16), trig.astype(np.float32)


def swap_blocks(tile):
    row = lax.broadcasted_iota(jnp.int32, (8, LANES), 0)
    block = lax.broadcasted_iota(jnp.int32, (8, LANES), 1) // BLOCK
    for bit in (1, 2, 4):
        row_set = (row & bit) != 0
        block_set = (block & bit) != 0
        up = pltpu.roll(pltpu.roll(tile, 8 - bit, 0), BLOCK * bit, 1)
        if bit == 4:
            tile = jnp.where(row_set == block_set, tile, up)
        else:
            down = pltpu.roll(pltpu.roll(tile, bit, 0), LANES - BLOCK * bit, 1)
            tile = jnp.where(row_set == block_set, tile, jnp.where(block_set, up, down))
    return tile


def kernel(
    s_hbm, p_hbm, target_hbm, cond_hbm, high_hbm, low_hbm, trig_hbm,
    rs_ref, rp_ref, got, own_cond, high_v, low_v, trig_v,
    s_v, p_v, w_v, target_v, cond_v,
    s_prev, p_next, edge_low, edge_high, from_low, from_high,
    blocks, cond_rows,
    load_sem, near_send, near_recv, block_send, block_recv, token, token_0, ready,
):
    tm = lax.axis_index("tm")
    space = lax.axis_index("space")
    group = lax.div(tm, OWNERS)
    rank = lax.rem(tm, OWNERS)
    later = lax.rem(tm + 1, STEPS)
    earlier = lax.rem(tm + STEPS - 1, STEPS)
    above = lax.rem(space + 1, 8)
    below = lax.rem(space + 7, 8)

    loads = [
        pltpu.make_async_copy(source, target, load_sem.at[i])
        for i, (source, target) in enumerate(
            (
                (s_hbm, s_v),
                (p_hbm, p_v),
                (cond_hbm, cond_v),
                (target_hbm, target_v),
                (high_hbm, high_v),
                (low_hbm, low_v),
                (trig_hbm, trig_v),
            )
        )
    ]
    x, y, z = lax.div(tm, 2 * DEPTH), lax.rem(tm, 2), lax.rem(lax.div(tm, 2), DEPTH)

    def at_plane(plane, j):
        return 2 * DEPTH * lax.rem(x + j // 2, 4) + 2 * plane + lax.rem(y + j, 2)

    def signal(semaphore, where):
        pl.semaphore_signal(semaphore, 1, device_id=where, device_id_type=pl.DeviceIdType.MESH)

    barrier = pltpu.get_barrier_semaphore()
    signal(barrier, {"space": above})
    signal(barrier, {"space": below})
    signal(barrier, {"tm": lax.rem(tm + STEPS - 1 + 2 * y, STEPS)})
    for load in loads[:3]:
        load.start()

    @pl.when(z > 0)
    def _():
        signal(barrier, {"tm": tm - 2})

    @pl.when(z < DEPTH - 1)
    def _():
        signal(barrier, {"tm": tm + 2})

    for j in range(1, 8):
        signal(barrier, {"tm": at_plane(z, j)})

    @pl.when((z >= HALF) & (space == 0))
    def _():
        signal(barrier, {"tm": 2 * DEPTH * x})

    @pl.when((z == 0) & (y == 0) & (space == 0))
    def _():
        for far in range(2 * HALF, 2 * DEPTH):
            signal(barrier, {"tm": tm + far})

    for load in loads[3:]:
        load.start()

    for load in loads[:3]:
        load.wait()
    for i in range(ROWS):
        w_v[i // 3, i % 3] = cond_v[i] * p_v[i // 3, i % 3]
    for edge, plane in ((edge_low, 0), (edge_high, 7)):
        for i in range(ROWS):
            edge[i : i + 1] = s_v[i // 3, i % 3, plane : plane + 1]
            edge[ROWS + i : ROWS + i + 1] = w_v[i // 3, i % 3, plane : plane + 1]

    last = DEPTH - 1
    greetings = 10 + (z + last - 1) // last + (2 * last - 1 - z) // last
    wrapped = (z + last - HALF) // last + 2 * (DEPTH - HALF) * (1 - y) * ((last - z) // last)
    greetings += wrapped * (1 - (space + 7) // 8)
    pl.semaphore_wait(barrier, greetings)

    def send(source, target, send_sem, recv_sem, where):
        copy = pltpu.make_async_remote_copy(
            src_ref=source, dst_ref=target, send_sem=send_sem, recv_sem=recv_sem,
            device_id=where, device_id_type=pl.DeviceIdType.MESH,
        )
        copy.start()
        return copy

    near = [
        send(edge_low, from_high, near_send.at[0], near_recv.at[0], {"space": below}),
        send(edge_high, from_low, near_send.at[1], near_recv.at[1], {"space": above}),
    ]
    for q in range(3):
        part, k = (slice(None), q), 2 + 2 * q
        near += [
            send(s_v.at[part], s_prev.at[part], near_send.at[k], near_recv.at[k], {"tm": later}),
            send(p_v.at[part], p_next.at[part], near_send.at[k + 1], near_recv.at[k + 1],
                 {"tm": earlier}),
        ]

    @pl.when(z > 1)
    def _():
        pl.semaphore_wait(token, 1)

    def hand_up(semaphore):
        signal(semaphore, {"tm": tm + 2})
        signal(semaphore, {"tm": tm + 1})

    @pl.when((y == 1) & (z > 0) & (z < DEPTH - 1))
    def _():
        hand_up(token)

    def announce(plane, carry):
        signal(ready, {"tm": at_plane(plane, 0)})
        return carry

    lax.fori_loop(1, z, announce, 0)

    @pl.when((z == 0) & (y == 0) & (space == 0))
    def _():
        for far in range(2 * HALF, 2 * DEPTH):
            signal(token_0, {"tm": tm + far})

    @pl.when(z > 0)
    def _():
        pl.semaphore_wait(token_0, 1)

    @pl.when((y == 1) & ((z < HALF - 1) | ((space > 0) & (z < DEPTH - 1))))
    def _():
        hand_up(token_0)

    @pl.when(z > 0)
    def _():
        signal(ready, {"tm": at_plane(0, 0)})

    cond_rows[...] = swap_blocks(cond_v[group])
    own_cond[...] = jnp.broadcast_to(cond_rows[pl.ds(rank, 1)], (LANES, LANES)).T

    row = lax.broadcasted_iota(jnp.int32, (8, LANES), 0)
    lane = lax.broadcasted_iota(jnp.int32, (8, LANES), 1)
    loads[3].wait()
    for copy in near[:2]:
        copy.wait_recv()

    def around(field, i, low, high):
        centre = field[i // 3, i % 3]
        low = jnp.broadcast_to(jnp.where(space == 0, 0.0, low), (8, LANES))
        high = jnp.broadcast_to(jnp.where(space == 7, 0.0, high), (8, LANES))
        z_low = jnp.where(row == 0, low, pltpu.roll(centre, 1, 0))
        z_high = jnp.where(row == 7, high, pltpu.roll(centre, 7, 0))
        y_low = jnp.where(lane == 0, 0.0, pltpu.roll(centre, 1, 1))
        y_high = jnp.where(lane == LANES - 1, 0.0, pltpu.roll(centre, LANES - 1, 1))
        total = (z_low + z_high) + (y_low + y_high)
        if i > 0:
            total += field[(i - 1) // 3, (i - 1) % 3]
        if i < ROWS - 1:
            total += field[(i + 1) // 3, (i + 1) % 3]
        return total

    mine = pl.ds(pl.multiple_of(2 * tm, 2), 2)

    def serve(plane, first):
        for j in range(first, 8):
            peer = at_plane(plane, j)
            theirs = pl.ds(pl.multiple_of(2 * peer, 2), 2)
            send(blocks.at[theirs], got.at[mine], block_send, block_recv, {"tm": peer})

    def serve_plane(plane, carry):
        serve(plane, 0)
        return carry

    def serve_lower(plane, carry):
        @pl.when(plane < z)
        def _():
            serve(plane, 0)

        return carry

    for i in range(ROWS):
        at = (i // 3, i % 3)
        s, p, w, cond = s_v[at], p_v[at], w_v[at], cond_v[i]
        around_s = around(s_v, i, from_low[i : i + 1], from_high[i : i + 1])
        around_w = around(
            w_v, i, from_low[ROWS + i : ROWS + i + 1], from_high[ROWS + i : ROWS + i + 1]
        )
        rs_ref[i] = s + diffusion * (cond * (6.0 * s - around_s)) - control_cost * p
        rp_ref[i] = p + diffusion * (6.0 * w - around_w) + tracking * (s - target_v[i])

    for q in range(3):
        for copy in near[2 + 2 * q : 4 + 2 * q]:
            copy.wait_recv()
        for i in range(q, ROWS, 3):
            rs = rs_ref[i] - s_prev[i // 3, q]
            rp = rp_ref[i] - p_next[i // 3, q]
            rs_ref[i] = rs
            rp_ref[i] = rp
            blocks[pl.ds(16 * i, 8, stride=2)] = swap_blocks(rs)
            blocks[pl.ds(16 * i + 1, 8, stride=2)] = swap_blocks(rp)
        lax.fori_loop(4 * q, 4 * q + 4, serve_lower, 0)

        @pl.when(lax.div(z, 4) == q)
        def _():
            serve(z, 1)

    own = pltpu.make_async_copy(blocks.at[mine], got.at[mine], block_recv)
    own.start()

    @pl.when(z < DEPTH - 1)
    def _():
        pl.semaphore_wait(ready, DEPTH - 1 - z)

    lax.fori_loop(z + 1, DEPTH, serve_plane, 0)
    for load in loads[4:]:
        load.wait()
    pltpu.make_async_copy(got, got, block_recv).wait()
    sent = blocks.at[pl.ds(0, TERMS - 2)]
    pltpu.make_async_copy(sent, sent, block_send).wait()
    for copy in near:
        copy.wait_send()


def solve(
    rs_ref, rp_ref, got, own_cond, high_v, low_v, trig_v,
    rs_hbm, rp_hbm, spec_hbm,
    spec_v, sem,
):
    copies = [
        pltpu.make_async_copy(rs_ref, rs_hbm, sem.at[0]),
        pltpu.make_async_copy(rp_ref, rp_hbm, sem.at[1]),
    ]
    for copy in copies:
        copy.start()
    def product(values, table):
        return lax.dot_general(
            values, table, (((0,), (0,)), ((), ())), preferred_element_type=jnp.float32
        )

    values = got[...]
    high = values.astype(jnp.bfloat16)
    low = (values - high.astype(jnp.float32)).astype(jnp.bfloat16)
    spectra = product(high, high_v[...]) + (product(high, low_v[...]) + product(low, high_v[...]))
    state_real, state_imag, adjoint_real, adjoint_imag = (
        spectra[:, LANES * i : LANES * (i + 1)] for i in range(4)
    )
    cosine, sine = trig_v[0:1], trig_v[1:2]
    diagonal = 1.0 + diffusion * 6.0 * own_cond[...] - cosine
    scale = 1.0 / (diagonal * diagonal + sine * sine + control_cost * tracking)
    fixes = (
        diagonal * state_real + sine * state_imag + control_cost * adjoint_real,
        diagonal * state_imag - sine * state_real + control_cost * adjoint_imag,
        diagonal * adjoint_real - sine * adjoint_imag - tracking * state_real,
        diagonal * adjoint_imag + sine * adjoint_real - tracking * state_imag,
    )
    for i, fix in enumerate(fixes):
        spec_v[i] = (fix * scale)[:, :STEPS]
        copy = pltpu.make_async_copy(spec_v.at[i], spec_hbm.at[i], sem.at[2 + i])
        copy.start()
        copies.append(copy)
    for copy in copies:
        copy.wait()


def shards(state_field, adjoint, target, conductivity):
    high, low, trig = dft_table()
    tiles = (ROWS, 8, LANES)
    parts = (ROWS // 3, 3, 8, LANES)
    stay = lambda array: pltpu.with_memory_space_constraint(array, pltpu.HBM)
    rows_first = lambda field: stay(jnp.transpose(field[0], (1, 0, 2)))
    in_parts = lambda field: stay(jnp.transpose(field[0], (1, 0, 2)).reshape(parts))
    vmem, dma = pltpu.VMEM, pltpu.SemaphoreType.DMA
    f32 = jnp.float32
    in_hbm = pl.BlockSpec(memory_space=pltpu.HBM)
    in_vmem = pl.BlockSpec(memory_space=pltpu.VMEM)
    rs, rp, got, own_cond, high, low, trig = pl.pallas_call(
        kernel,
        out_shape=(
            jax.ShapeDtypeStruct(tiles, f32),
            jax.ShapeDtypeStruct(tiles, f32),
            jax.ShapeDtypeStruct((TERMS, LANES), f32),
            jax.ShapeDtypeStruct((LANES, LANES), f32),
            jax.ShapeDtypeStruct((TERMS, 4 * LANES), jnp.bfloat16),
            jax.ShapeDtypeStruct((TERMS, 4 * LANES), jnp.bfloat16),
            jax.ShapeDtypeStruct((8, LANES), f32),
        ),
        in_specs=[in_hbm] * 7,
        out_specs=(in_vmem,) * 7,
        scratch_shapes=[
            vmem(parts, f32),
            vmem(parts, f32),
            vmem(parts, f32),
            vmem(tiles, f32),
            vmem(tiles, f32),
            vmem(parts, f32),
            vmem(parts, f32),
            vmem((2 * ROWS, LANES), f32),
            vmem((2 * ROWS, LANES), f32),
            vmem((2 * ROWS, LANES), f32),
            vmem((2 * ROWS, LANES), f32),
            vmem((TERMS, LANES), f32),
            vmem((8, LANES), f32),
            dma((7,)),
            dma((8,)),
            dma((8,)),
            dma,
            dma,
            pltpu.SemaphoreType.REGULAR,
            pltpu.SemaphoreType.REGULAR,
            pltpu.SemaphoreType.REGULAR,
        ],
        compiler_params=pltpu.CompilerParams(
            collective_id=0, has_side_effects=True, vmem_limit_bytes=24 * 1024 * 1024
        ),
    )(
        in_parts(state_field), in_parts(adjoint), rows_first(target),
        stay(jnp.transpose(conductivity, (1, 0, 2))),
        stay(jnp.asarray(high)), stay(jnp.asarray(low)), stay(jnp.asarray(trig)),
    )
    rs, rp, spec = pl.pallas_call(
        solve,
        out_shape=(
            jax.ShapeDtypeStruct(tiles, f32),
            jax.ShapeDtypeStruct(tiles, f32),
            jax.ShapeDtypeStruct((4, LANES, STEPS), f32),
        ),
        in_specs=[in_vmem] * 7,
        out_specs=(in_hbm,) * 3,
        scratch_shapes=[vmem((4, LANES, STEPS), f32), dma((6,))],
        compiler_params=pltpu.CompilerParams(vmem_limit_bytes=16 * 1024 * 1024),
    )(rs, rp, got, own_cond, high, low, trig)
    back = lambda tile: jnp.transpose(tile, (1, 0, 2))[None]
    spectral = jnp.transpose(spec.reshape(4, 8, BLOCK, STEPS), (0, 3, 1, 2))
    return back(rs), back(rp), spectral


def solution(mesh):
    placed = (
        P("tm", "space", None, None),
        P("tm", "space", None, None),
        P("tm", "space", None, None),
        P("space", None, None),
    )
    return jax.shard_map(
        shards,
        mesh=mesh,
        in_specs=placed,
        out_specs=(
            P("tm", "space", None, None),
            P("tm", "space", None, None),
            P(None, None, "space", "tm"),
        ),
        check_vma=False,
    )
```

time: 32 us -> 29.7 us (0.928)
  the two profiles are of different devices: /device:TPU:8 before, /device:TPU:1 now
where the time goes in v5:
time: 29.7 us; the launch traced here: 29.2 us
  Pallas kernels  28.6 us (96%)
  between operations  0.64 us (2%)
    pallas_call x1, Pallas kernels, shards(): pl.pallas_call(kernel, out_shape=(jax.ShapeDtypeStruct(tiles, f32), jax.S...  27.5 us
    pallas_call x1, Pallas kernels, shards(): pl.pallas_call(solve, out_shape=(jax.ShapeDtypeStruct(tiles, f32), jax.Sh...  1.07 us

profile of v5, /device:TPU:1, one launch (start us, length us, event | category | flops | bytes accessed | tf_op | source)
XLA Modules:
  0.0 29.2 jit_solution(6477415359322457767)
XLA Ops:
  0.6 27.5 %shard_map.94 = (f32[12,8,128]{2,1,0:T(8,128)S(1)}, f32[12,8,128]{2,1,0:T(8,128)S(1)}, f32[192,128]{1,0:T(8,128)S(1)}, f32[128,128]{1,0:T(8,128)S(1)}, bf16[192,...) custom-call(f32[4,3,8,128]{3,2,1,0:T(8,128)} %bitcast.23, f32[4,3,8,128]{3,2,1,0:T(8,128)} %bitcast.24, ...), custom_call_target="tpu_custom_call" | custom-call | tf_op jit(solution)/shard_map/pallas_call | solution.py:334
  28.1 1.1 %shard_map.95 = (f32[12,8,128]{2,1,0:T(8,128)}, f32[12,8,128]{2,1,0:T(8,128)}, f32[4,128,96]{2,1,0:T(8,128)}) custom-call(f32[12,8,128]{2,1,0:T(8,128)S(1)} %get-tuple-element.13.rs_ref, f32[12,8,128]{2,1,0:T(8,128)S(1)} %get-tuple-element.14.rp_ref, f32[192,128]{1,0:T(8,128)S(1)} %get-tuple-element.15.got, f32[128,128]{1,0:T(8,128)S(1)} %get-tuple-element.16.own_cond, ...), custom_call_target="tpu_custom_call" | custom-call | tf_op jit(solution)/shard_map/pallas_call | solution.py:378

commit v6 on v5

--- a/solution.py
+++ b/solution.py
@@ -97,20 +97,17 @@
     signal(barrier, {"space": above})
     signal(barrier, {"space": below})
     signal(barrier, {"tm": lax.rem(tm + STEPS - 1 + 2 * y, STEPS)})
-    for load in loads[:3]:
-        load.start()
-
-    @pl.when(z > 0)
-    def _():
-        signal(barrier, {"tm": tm - 2})
-
-    @pl.when(z < DEPTH - 1)
-    def _():
-        signal(barrier, {"tm": tm + 2})
-
     for j in range(1, 8):
         signal(barrier, {"tm": at_plane(z, j)})
 
+    @pl.when(z > 0)
+    def _():
+        signal(barrier, {"tm": tm - 2})
+
+    @pl.when(z < DEPTH - 1)
+    def _():
+        signal(barrier, {"tm": tm + 2})
+
     @pl.when((z >= HALF) & (space == 0))
     def _():
         signal(barrier, {"tm": 2 * DEPTH * x})
@@ -120,7 +117,7 @@
         for far in range(2 * HALF, 2 * DEPTH):
             signal(barrier, {"tm": tm + far})
 
-    for load in loads[3:]:
+    for load in loads:
         load.start()
 
     for load in loads[:3]:
@@ -138,6 +135,11 @@
     greetings += wrapped * (1 - (space + 7) // 8)
     pl.semaphore_wait(barrier, greetings)
 
+    @pl.when((z == 0) & (y == 0) & (space == 0))
+    def _():
+        for far in range(2 * HALF, 2 * DEPTH):
+            signal(token_0, {"tm": tm + far})
+
     def send(source, target, send_sem, recv_sem, where):
         copy = pltpu.make_async_remote_copy(
             src_ref=source, dst_ref=target, send_sem=send_sem, recv_sem=recv_sem,
@@ -146,18 +148,20 @@
         copy.start()
         return copy
 
-    near = [
-        send(edge_low, from_high, near_send.at[0], near_recv.at[0], {"space": below}),
-        send(edge_high, from_low, near_send.at[1], near_recv.at[1], {"space": above}),
-    ]
-    for q in range(3):
+    def send_part(q):
         part, k = (slice(None), q), 2 + 2 * q
-        near += [
+        return [
             send(s_v.at[part], s_prev.at[part], near_send.at[k], near_recv.at[k], {"tm": later}),
             send(p_v.at[part], p_next.at[part], near_send.at[k + 1], near_recv.at[k + 1],
                  {"tm": earlier}),
         ]
 
+    first_part = send_part(0)
+    near = [
+        send(edge_low, from_high, near_send.at[0], near_recv.at[0], {"space": below}),
+        send(edge_high, from_low, near_send.at[1], near_recv.at[1], {"space": above}),
+    ] + first_part + send_part(1) + send_part(2)
+
     @pl.when(z > 1)
     def _():
         pl.semaphore_wait(token, 1)
@@ -175,11 +179,6 @@
         return carry
 
     lax.fori_loop(1, z, announce, 0)
-
-    @pl.when((z == 0) & (y == 0) & (space == 0))
-    def _():
-        for far in range(2 * HALF, 2 * DEPTH):
-            signal(token_0, {"tm": tm + far})
 
     @pl.when(z > 0)
     def _():

time: 29.7 us -> 29.7 us (level)
  no operation moved by 1% of the time
where the time goes in v6:
time: 29.7 us; the launch traced here: 29.4 us
  Pallas kernels  28.7 us (97%)
  between operations  0.64 us (2%)
    pallas_call x1, Pallas kernels, shards(): pl.pallas_call(kernel, out_shape=(jax.ShapeDtypeStruct(tiles, f32), jax.S...  27.7 us
    pallas_call x1, Pallas kernels, shards(): pl.pallas_call(solve, out_shape=(jax.ShapeDtypeStruct(tiles, f32), jax.Sh...  1.06 us

profile of v6, /device:TPU:1, one launch (start us, length us, event | category | flops | bytes accessed | tf_op | source)
XLA Modules:
  0.0 29.4 jit_solution(17985143096653118616)
XLA Ops:
  0.6 27.7 %shard_map.94 = (f32[12,8,128]{2,1,0:T(8,128)S(1)}, f32[12,8,128]{2,1,0:T(8,128)S(1)}, f32[192,128]{1,0:T(8,128)S(1)}, f32[128,128]{1,0:T(8,128)S(1)}, bf16[192,...) custom-call(f32[4,3,8,128]{3,2,1,0:T(8,128)} %bitcast.23, f32[4,3,8,128]{3,2,1,0:T(8,128)} %bitcast.24, ...), custom_call_target="tpu_custom_call" | custom-call | tf_op jit(solution)/shard_map/pallas_call | solution.py:333
  28.3 1.1 %shard_map.95 = (f32[12,8,128]{2,1,0:T(8,128)}, f32[12,8,128]{2,1,0:T(8,128)}, f32[4,128,96]{2,1,0:T(8,128)}) custom-call(f32[12,8,128]{2,1,0:T(8,128)S(1)} %get-tuple-element.13.rs_ref, f32[12,8,128]{2,1,0:T(8,128)S(1)} %get-tuple-element.14.rp_ref, f32[192,128]{1,0:T(8,128)S(1)} %get-tuple-element.15.got, f32[128,128]{1,0:T(8,128)S(1)} %get-tuple-element.16.own_cond, ...), custom_call_target="tpu_custom_call" | custom-call | tf_op jit(solution)/shard_map/pallas_call | solution.py:377

commit v7 on v6

--- a/solution.py
+++ b/solution.py
@@ -174,23 +174,23 @@
     def _():
         hand_up(token)
 
+    @pl.when(z > 0)
+    def _():
+        pl.semaphore_wait(token_0, 1)
+
+    @pl.when((y == 1) & ((z < HALF - 1) | ((space > 0) & (z < DEPTH - 1))))
+    def _():
+        hand_up(token_0)
+
+    @pl.when(z > 0)
+    def _():
+        signal(ready, {"tm": at_plane(0, 0)})
+
     def announce(plane, carry):
         signal(ready, {"tm": at_plane(plane, 0)})
         return carry
 
     lax.fori_loop(1, z, announce, 0)
-
-    @pl.when(z > 0)
-    def _():
-        pl.semaphore_wait(token_0, 1)
-
-    @pl.when((y == 1) & ((z < HALF - 1) | ((space > 0) & (z < DEPTH - 1))))
-    def _():
-        hand_up(token_0)
-
-    @pl.when(z > 0)
-    def _():
-        signal(ready, {"tm": at_plane(0, 0)})
 
     cond_rows[...] = swap_blocks(cond_v[group])
     own_cond[...] = jnp.broadcast_to(cond_rows[pl.ds(rank, 1)], (LANES, LANES)).T
@@ -219,7 +219,7 @@
     mine = pl.ds(pl.multiple_of(2 * tm, 2), 2)
 
     def serve(plane, first):
-        for j in range(first, 8):
+        for j in (5, 4, 7, 3, 6, 2, 1, 0)[: 8 - first]:
             peer = at_plane(plane, j)
             theirs = pl.ds(pl.multiple_of(2 * peer, 2), 2)
             send(blocks.at[theirs], got.at[mine], block_send, block_recv, {"tm": peer})

time: 29.7 us -> 29.7 us (level)
  no operation moved by 1% of the time
where the time goes in v7:
time: 29.7 us; the launch traced here: 29.4 us
  Pallas kernels  28.7 us (97%)
  between operations  0.64 us (2%)
    pallas_call x1, Pallas kernels, shards(): pl.pallas_call(kernel, out_shape=(jax.ShapeDtypeStruct(tiles, f32), jax.S...  27.7 us
    pallas_call x1, Pallas kernels, shards(): pl.pallas_call(solve, out_shape=(jax.ShapeDtypeStruct(tiles, f32), jax.Sh...  1.06 us

profile of v7, /device:TPU:1, one launch (start us, length us, event | category | flops | bytes accessed | tf_op | source)
XLA Modules:
  0.0 29.4 jit_solution(18015948789203574299)
XLA Ops:
  0.6 27.7 %shard_map.94 = (f32[12,8,128]{2,1,0:T(8,128)S(1)}, f32[12,8,128]{2,1,0:T(8,128)S(1)}, f32[192,128]{1,0:T(8,128)S(1)}, f32[128,128]{1,0:T(8,128)S(1)}, bf16[192,...) custom-call(f32[4,3,8,128]{3,2,1,0:T(8,128)} %bitcast.23, f32[4,3,8,128]{3,2,1,0:T(8,128)} %bitcast.24, ...), custom_call_target="tpu_custom_call" | custom-call | tf_op jit(solution)/shard_map/pallas_call | solution.py:333
  28.3 1.1 %shard_map.95 = (f32[12,8,128]{2,1,0:T(8,128)}, f32[12,8,128]{2,1,0:T(8,128)}, f32[4,128,96]{2,1,0:T(8,128)}) custom-call(f32[12,8,128]{2,1,0:T(8,128)S(1)} %get-tuple-element.13.rs_ref, f32[12,8,128]{2,1,0:T(8,128)S(1)} %get-tuple-element.14.rp_ref, f32[192,128]{1,0:T(8,128)S(1)} %get-tuple-element.15.got, f32[128,128]{1,0:T(8,128)S(1)} %get-tuple-element.16.own_cond, ...), custom_call_target="tpu_custom_call" | custom-call | tf_op jit(solution)/shard_map/pallas_call | solution.py:377

commit v8 on v7

--- a/solution.py
+++ b/solution.py
@@ -100,11 +100,11 @@
     for j in range(1, 8):
         signal(barrier, {"tm": at_plane(z, j)})
 
-    @pl.when(z > 0)
+    @pl.when((y == 1) & (z > 0))
     def _():
         signal(barrier, {"tm": tm - 2})
 
-    @pl.when(z < DEPTH - 1)
+    @pl.when((y == 1) & (z < DEPTH - 1))
     def _():
         signal(barrier, {"tm": tm + 2})
 
@@ -130,7 +130,7 @@
             edge[ROWS + i : ROWS + i + 1] = w_v[i // 3, i % 3, plane : plane + 1]
 
     last = DEPTH - 1
-    greetings = 10 + (z + last - 1) // last + (2 * last - 1 - z) // last
+    greetings = 10 + y * ((z + last - 1) // last + (2 * last - 1 - z) // last)
     wrapped = (z + last - HALF) // last + 2 * (DEPTH - HALF) * (1 - y) * ((last - z) // last)
     greetings += wrapped * (1 - (space + 7) // 8)
     pl.semaphore_wait(barrier, greetings)

time: 29.7 us -> 29.7 us (level)
  no operation moved by 1% of the time
where the time goes in v8:
time: 29.7 us; the launch traced here: 29.4 us
  Pallas kernels  28.7 us (97%)
  between operations  0.64 us (2%)
    pallas_call x1, Pallas kernels, shards(): pl.pallas_call(kernel, out_shape=(jax.ShapeDtypeStruct(tiles, f32), jax.S...  27.7 us
    pallas_call x1, Pallas kernels, shards(): pl.pallas_call(solve, out_shape=(jax.ShapeDtypeStruct(tiles, f32), jax.Sh...  1.07 us

profile of v8, /device:TPU:1, one launch (start us, length us, event | category | flops | bytes accessed | tf_op | source)
XLA Modules:
  0.0 29.4 jit_solution(17212957251006919794)
XLA Ops:
  0.6 27.7 %shard_map.94 = (f32[12,8,128]{2,1,0:T(8,128)S(1)}, f32[12,8,128]{2,1,0:T(8,128)S(1)}, f32[192,128]{1,0:T(8,128)S(1)}, f32[128,128]{1,0:T(8,128)S(1)}, bf16[192,...) custom-call(f32[4,3,8,128]{3,2,1,0:T(8,128)} %bitcast.23, f32[4,3,8,128]{3,2,1,0:T(8,128)} %bitcast.24, ...), custom_call_target="tpu_custom_call" | custom-call | tf_op jit(solution)/shard_map/pallas_call | solution.py:333
  28.3 1.1 %shard_map.95 = (f32[12,8,128]{2,1,0:T(8,128)}, f32[12,8,128]{2,1,0:T(8,128)}, f32[4,128,96]{2,1,0:T(8,128)}) custom-call(f32[12,8,128]{2,1,0:T(8,128)S(1)} %get-tuple-element.13.rs_ref, f32[12,8,128]{2,1,0:T(8,128)S(1)} %get-tuple-element.14.rp_ref, f32[192,128]{1,0:T(8,128)S(1)} %get-tuple-element.15.got, f32[128,128]{1,0:T(8,128)S(1)} %get-tuple-element.16.own_cond, ...), custom_call_target="tpu_custom_call" | custom-call | tf_op jit(solution)/shard_map/pallas_call | solution.py:377
